TPU v7x, 128 devices: a whole 4x4x4 slice. The times are simulated.
128 devices in a mesh: seq: 4 (over x_hi, core), res: 32 (over z, x_lo, y).
Axes of the slice: x: 4 (x_hi: 2, x_lo: 2; x = x_hi * 2 + x_lo), y: 4, z: 4, core: 2. Of those that a mesh axis runs over, the one named last changes fastest.
Arguments:
- normed_homolog_matrix: bfloat16 [4, 4096, 256], P('seq', 'res'), may hold values from -6 to 6
- result_cotangent: bfloat16 [4, 4096, 256], P('seq', 'res'), may hold values from -16 to 16
- question_matrix: bfloat16 [256, 256], replicated, may hold values from -0.375 to 0.375
- lookup_matrix: bfloat16 [256, 256], replicated, may hold values from -0.375 to 0.375
- content_matrix: bfloat16 [256, 256], replicated, may hold values from -0.375 to 0.375
- sigmoid_matrix: bfloat16 [256, 256], replicated, may hold values from -0.375 to 0.375
- result_matrix: bfloat16 [256, 256], replicated, may hold values from -0.375 to 0.375
- residue_pair_bias: bfloat16 [8, 4096, 4096], P(None, 'seq', 'res'), may hold values from -240 to 240
Outputs:
- homolog_derivative: bfloat16 [4, 4096, 256], P('seq', 'res')
- couple_offset_derivative: float32 [8, 4096, 4096], P(None, 'seq', 'res')
All inputs are finite; a program needn't handle non-finite values.
Results may differ from a plain program's by a relative error of at most 0.028.
Values may be sent and summed in bfloat16 or wider, within the bound.
A program may use at most 192 MiB of HBM per device.

v0:
```python
import jax
import jax.numpy as jnp
from jax import lax
from jax.sharding import PartitionSpec as P


def reduced_width(values):
    return values.astype(jnp.bfloat16)


def linear_map(rows, weight, number_heads):
    flat_rows = rows.reshape(-1, rows.shape[-1])
    result = jnp.dot(flat_rows, weight, preferred_element_type=jnp.float32)
    return result.reshape(rows.shape[0], rows.shape[1], number_heads, -1)


def attend(
    query_alignment,
    query_adjoint,
    bias_row_slices,
    gathered_key_rows,
    gathered_value_rows,
    question_matrix,
    sigmoid_matrix,
    result_matrix,
    number_heads,
):
    number_sequences, number_queries, total_width = query_alignment.shape
    key_count = gathered_key_rows.shape[1]
    head_size = total_width // number_heads
    query_scaling = head_size ** (-0.5)
    query_vectors = reduced_width(
        linear_map(query_alignment, question_matrix, number_heads) * query_scaling
    )
    gate_preactivation = linear_map(query_alignment, sigmoid_matrix, number_heads)
    sigmoid_derivative = linear_map(query_adjoint, result_matrix.T, number_heads)
    keys_split = gathered_key_rows.reshape(number_sequences, key_count, number_heads, head_size)
    values_split = gathered_value_rows.reshape(number_sequences, key_count, number_heads, head_size)
    block_size = min(512, key_count)
    block_total = key_count // block_size
    block_starts = jnp.arange(block_total, dtype=jnp.int32) * block_size

    def block_scores(row_start):
        key_block = lax.dynamic_slice_in_dim(keys_split, row_start, block_size, 1)
        value_block = lax.dynamic_slice_in_dim(values_split, row_start, block_size, 1)
        bias_block = lax.dynamic_slice_in_dim(bias_row_slices, row_start, block_size, 2)
        scores = jnp.einsum(
            "bihd,bjhd->bhij", query_vectors, key_block, preferred_element_type=jnp.float32
        )
        return (scores + bias_block[None].astype(jnp.float32), key_block, value_block)

    def stats_step(running, row_start):
        row_top, exp_total = running
        scores = block_scores(row_start)[0]
        new_top = jnp.maximum(row_top, jnp.max(scores, -1))
        exp_total = exp_total * jnp.exp(row_top - new_top) + jnp.sum(
            jnp.exp(scores - new_top[..., None]), -1
        )
        return ((new_top, exp_total), None)

    stat_shape = (number_sequences, number_heads, number_queries)
    start_state = (jnp.full(stat_shape, -jnp.inf, jnp.float32), jnp.zeros(stat_shape, jnp.float32))
    final_stats = lax.scan(stats_step, start_state, block_starts)[0]
    log_total = (final_stats[0] + jnp.log(final_stats[1]))[..., None]

    def output_step(attn_acc, row_start):
        scores, key_block, value_block = block_scores(row_start)
        prob_low = reduced_width(jnp.exp(scores - log_total))
        attn_acc = attn_acc + jnp.einsum(
            "bhij,bjhd->bihd", prob_low, value_block, preferred_element_type=jnp.float32
        )
        return (attn_acc, None)

    out_shape = (number_sequences, number_queries, number_heads, head_size)
    attn_out = lax.scan(output_step, jnp.zeros(out_shape, jnp.float32), block_starts)[0]
    gate_open = jax.nn.sigmoid(gate_preactivation)
    attn_grad = reduced_width(sigmoid_derivative * gate_open)
    logit_grad = reduced_width(sigmoid_derivative * attn_out * gate_open * (1.0 - gate_open))
    row_dot = jnp.transpose(jnp.sum(attn_grad.astype(jnp.float32) * attn_out, -1), (0, 2, 1))[
        ..., None
    ]

    def grad_step(query_acc, row_start):
        scores, key_block, value_block = block_scores(row_start)
        attn_probs = jnp.exp(scores - log_total)
        prob_low = reduced_width(attn_probs)
        prob_grad = jnp.einsum(
            "bihd,bjhd->bhij", attn_grad, value_block, preferred_element_type=jnp.float32
        )
        score_grad = attn_probs * (prob_grad - row_dot)
        score_low = reduced_width(score_grad)
        query_acc = query_acc + jnp.einsum(
            "bhij,bjhd->bihd", score_low, key_block, preferred_element_type=jnp.float32
        )
        key_term = jnp.einsum(
            "bhij,bihd->bjhd", score_low, query_vectors, preferred_element_type=jnp.float32
        )
        value_term = jnp.einsum(
            "bhij,bihd->bjhd", prob_low, attn_grad, preferred_element_type=jnp.float32
        )
        bias_term = reduced_width(jnp.sum(score_grad, 0))
        return (query_acc, (key_term, value_term, bias_term))

    query_acc, block_terms = lax.scan(grad_step, jnp.zeros(out_shape, jnp.float32), block_starts)
    key_terms = jnp.transpose(block_terms[0], (1, 0, 2, 3, 4)).reshape(
        number_sequences, key_count, total_width
    )
    value_terms = jnp.transpose(block_terms[1], (1, 0, 2, 3, 4)).reshape(
        number_sequences, key_count, total_width
    )
    bias_part = jnp.transpose(block_terms[2], (1, 2, 0, 3)).reshape(
        number_heads, number_queries, key_count
    )
    query_low = reduced_width(query_acc * query_scaling)
    query_partner = jnp.dot(
        query_low.reshape(-1, total_width), question_matrix.T, preferred_element_type=jnp.float32
    )
    query_partner = query_partner + jnp.dot(
        logit_grad.reshape(-1, total_width), sigmoid_matrix.T, preferred_element_type=jnp.float32
    )
    return (
        query_partner.reshape(number_sequences, number_queries, total_width),
        key_terms,
        value_terms,
        bias_part,
    )


def on_device(
    normed_homolog_matrix,
    result_cotangent,
    question_matrix,
    lookup_matrix,
    content_matrix,
    sigmoid_matrix,
    result_matrix,
    residue_pair_bias,
):
    number_sequences, residues_shard, total_width = normed_homolog_matrix.shape
    number_heads, tile_rows, tile_cols = residue_pair_bias.shape
    local_key_rows = reduced_width(
        linear_map(normed_homolog_matrix, lookup_matrix, number_heads)
    ).reshape(number_sequences, residues_shard, total_width)
    local_value_rows = reduced_width(
        linear_map(normed_homolog_matrix, content_matrix, number_heads)
    ).reshape(number_sequences, residues_shard, total_width)
    gathered_key_rows, gathered_value_rows = (
        lax.all_gather(local_key_rows, "res", axis=1, tiled=True),
        lax.all_gather(local_value_rows, "res", axis=1, tiled=True),
    )
    bias_cols = lax.all_gather(residue_pair_bias, "seq", axis=1, tiled=True)
    bias_row_slices = lax.all_to_all(bias_cols, "res", split_axis=1, concat_axis=2, tiled=True)
    query_partner, key_terms, value_terms, bias_part = attend(
        normed_homolog_matrix,
        result_cotangent,
        bias_row_slices,
        gathered_key_rows,
        gathered_value_rows,
        question_matrix,
        sigmoid_matrix,
        result_matrix,
        number_heads,
    )
    moved_rows = lax.all_to_all(bias_part, "res", split_axis=2, concat_axis=1, tiled=True)
    couple_offset_derivative = lax.psum_scatter(
        moved_rows.astype(jnp.float32).astype(jnp.bfloat16), "seq", scatter_dimension=1, tiled=True
    ).astype(jnp.float32)
    lookup_derivative, content_derivative = (
        lax.psum_scatter(
            key_terms.astype(jnp.bfloat16), "res", scatter_dimension=1, tiled=True
        ).astype(jnp.float32),
        lax.psum_scatter(
            value_terms.astype(jnp.bfloat16), "res", scatter_dimension=1, tiled=True
        ).astype(jnp.float32),
    )
    key_partner = jnp.dot(
        reduced_width(lookup_derivative).reshape(-1, total_width),
        lookup_matrix.T,
        preferred_element_type=jnp.float32,
    )
    key_partner = key_partner + jnp.dot(
        reduced_width(content_derivative).reshape(-1, total_width),
        content_matrix.T,
        preferred_element_type=jnp.float32,
    )
    homolog_derivative = (
        query_partner + key_partner.reshape(number_sequences, residues_shard, total_width)
    ).astype(jnp.bfloat16)
    return (homolog_derivative, couple_offset_derivative)


def solution(mesh):
    return jax.shard_map(
        on_device,
        mesh=mesh,
        in_specs=(
            P("seq", "res", None),
            P("seq", "res", None),
            P(),
            P(),
            P(),
            P(),
            P(),
            P(None, "seq", "res"),
        ),
        out_specs=(P("seq", "res", None), P(None, "seq", "res")),
        check_vma=False,
    )
```

profile of v0, /device:TPU:1, one launch (start us, length us, event | category | flops | bytes accessed | tf_op | source)
XLA Modules:
  0.0 1022.1 jit_solution(17029329577088041945)
XLA Ops:
  8.1 4.3 copy.78
  12.4 66.0 %all-gather.6.cloned.1.call-done = bf16[8,4096,128]{2,0,1:T(8,128)(2,1)} async-done(((bf16[8,1024,128]{2,0,1:T(8,128)(2,1)}), bf16[8,4096,128]{2,0,1:T(8,128)(2,1)}) %all-gather.6.cloned.1.call-update) | async-done | bytes 8388624 | tf_op jit(solution)/shard_map/all_gather | solution.py:151
  78.5 7.1 all-to-all-start
  88.4 114.8 %all-to-all-done = bf16[8,4096,128]{2,0,1:T(8,128)(2,1)} async-done(((bf16[8,4096,128]{2,0,1:T(8,128)(2,1)}), bf16[8,4096,128]{2,0,1:T(8,128)(2,1)}, u32[]{:S(2)}, u32[]{:S(2)}) %all-to-all-start) | async-done | bytes 8388640 | tf_op jit(solution)/shard_map/all_to_all | solution.py:152
  203.2 12.4 %copy.79 = bf16[8,128,32,128]{1,3,2,0:T(8,128)(2,1)} copy(bf16[8,128,32,128]{3,0,1,2:T(8,128)(2,1)} %bitcast.10) | data formatting | bytes 16777216 | tf_op jit(solution)/shard_map/all_to_all | solution.py:152
  215.6 65.4 %all-gather.4.cloned.1.call-done = bf16[1,4096,256]{1,2,0:T(8,128)(2,1)} async-done(((bf16[1,128,256]{1,2,0:T(8,128)(2,1)}), bf16[1,4096,256]{1,2,0:T(8,128)(2,1)}) %all-gather.4.cloned.1.call-update) | async-done | bytes 2097168 | tf_op jit(solution)/shard_map/all_gather | solution.py:148
  281.0 40.2 %while.41 = (s32[]{:T(128)}, f32[1,8,128]{2,1,0:T(8,128)S(1)}, f32[1,8,128]{2,1,0:T(8,128)S(1)}, s32[8]{0:T(128)S(1)}, bf16[1,4096,8,32]{1,3,2,0:T(8,128)(2,1)},...) while((s32[]{:T(128)}, f32[1,8,128]{2,1,0:T(8,128)S(1)}, ...), condition=%wide.region_3.4_spmd.clone, body=%wide.region_0.3_spmd.clone.sunk | while | flops 36180996 | bytes 5624998 | solution.py:63
  321.3 83.3 %all-gather.8.cloned.1.call-done = bf16[1,4096,256]{1,2,0:T(8,128)(2,1)} async-done(((bf16[1,128,256]{1,2,0:T(8,128)(2,1)}), bf16[1,4096,256]{1,2,0:T(8,128)(2,1)}) %all-gather.8.cloned.1.call-update) | async-done | bytes 2097168 | tf_op jit(solution)/shard_map/all_gather | solution.py:149
  404.6 40.6 %while.42 = (s32[]{:T(128)}, f32[1,128,8,32]{1,3,2,0:T(8,128)S(1)}, s32[8]{0:T(128)S(1)}, bf16[1,4096,8,32]{1,3,2,0:T(8,128)(2,1)}, bf16[1,4096,8,32]{1,3,2,0:T(...) while((s32[]{:T(128)}, f32[1,128,8,32]{1,3,2,0:T(8,128)S(1)}, ...), condition=%wide.region_5.6_spmd.clone, body=%wide.region_4.5_spmd.clone.sunk | while | flops 69271560 | bytes 1906860 | solution.py:75
  445.5 83.2 %while.43 = (s32[]{:T(128)}, f32[1,128,8,32]{1,3,2,0:T(8,128)S(1)}, bf16[8,1,512,8,32]{2,4,3,1,0:T(8,128)(2,1)S(1)}, bf16[8,1,512,8,32]{2,4,3,1,0:T(8,128)(2,1)}...) while((s32[]{:T(128)}, f32[1,128,8,32]{1,3,2,0:T(8,128)S(1)}, ...), condition=%wide.region_8.0_spmd.clone, body=%wide.region_7.8_spmd.clone.sunk | while | flops 171507712 | bytes 13903081 | solution.py:104
  531.3 2.9 convert_element_type.112
  534.1 7.1 copy.96
  541.2 3.9 copy.107
  545.1 10.4 %copy.87 = bf16[8,128,4096]{1,0,2:T(8,128)(2,1)} copy(bf16[8,128,4096]{1,2,0:T(8,128)(2,1)} %bitcast.291) | data formatting | bytes 16777216 | tf_op jit(solution)/shard_map/reshape | solution.py:111
  555.5 5.9 all-to-all-start.1
  564.0 2.9 convert_element_type.114
  566.9 7.1 copy.98
  574.0 3.9 copy.106
  577.9 84.4 %all-to-all-done.1 = bf16[8,128,4096]{1,0,2:T(8,128)(2,1)} async-done(((bf16[8,128,4096]{1,0,2:T(8,128)(2,1)}), bf16[8,128,4096]{1,0,2:T(8,128)(2,1)}, u32[]{:S(2)}, u32[]{:S(2)}) %all-to-all-start.1) | async-done | bytes 8388640 | tf_op jit(solution)/shard_map/all_to_all | solution.py:164
  662.3 12.4 %copy.89 = bf16[8,32,128,128]{3,2,1,0:T(8,128)(2,1)} copy(bf16[8,32,128,128]{2,0,3,1:T(8,128)(2,1)} %bitcast.37) | data formatting | bytes 16777216 | tf_op jit(solution)/shard_map/all_to_all | solution.py:164
  674.9 76.1 %reduce-scatter.10.cloned.1.call-done = bf16[128,256]{1,0:T(8,128)(2,1)} async-done(((bf16[4096,256]{1,0:T(8,128)(2,1)}), bf16[128,256]{1,0:T(8,128)(2,1)}) %reduce-scatter.10.cloned.1.call-update) | async-done | bytes 65552
  752.1 157.0 %reduce-scatter.12.cloned.1.call-done = bf16[128,256]{1,0:T(8,128)(2,1)} async-done(((bf16[4096,256]{1,0:T(8,128)(2,1)}), bf16[128,256]{1,0:T(8,128)(2,1)}) %reduce-scatter.12.cloned.1.call-update) | async-done | bytes 65552
  911.4 99.2 %reduce-scatter.8.cloned.1.call-done = bf16[8,1024,128]{2,1,0:T(8,128)(2,1)} async-done(((bf16[8,4096,128]{2,1,0:T(8,128)(2,1)}), bf16[8,1024,128]{2,1,0:T(8,128)(2,1)}) %reduce-scatter.8.cloned.1.call-update) | async-done | bytes 2097168 | tf_op jit(solution)/shard_map/reduce_scatter | solution.py:165
  1010.7 3.9 convert_element_type.117
  (171 shorter events, 128.5 us)
Async XLA Ops:
  8.0 80.2 %copy-start = (bf16[256,256]{1,0:T(8,128)(2,1)S(1)}, bf16[256,256]{1,0:T(8,128)(2,1)}, u32[]{:S(2)}) copy-start(bf16[256,256]{1,0:T(8,128)(2,1)} %param.20) | copy-start | bytes 393220
  8.0 70.5 %all-gather.6.cloned.1.call-start = ((), (), s32[]{:S(2)}) async-start(), calls=%async_computation.6 | async-start | bytes 10485760 | tf_op jit(solution)/shard_map/all_gather | solution.py:151
  12.4 73.3 %copy-start.6 = (bf16[256,256]{1,0:T(8,128)(2,1)S(1)}, bf16[256,256]{1,0:T(8,128)(2,1)}, u32[]{:S(2)}) copy-start(bf16[256,256]{1,0:T(8,128)(2,1)} %param.17) | copy-start | bytes 393220
  12.4 73.4 %copy-start.3 = (bf16[1,128,256]{2,1,0:T(8,128)(2,1)S(1)}, bf16[1,128,256]{2,1,0:T(8,128)(2,1)}, u32[]{:S(2)}) copy-start(bf16[1,128,256]{2,1,0:T(8,128)(2,1)} %param.14) | copy-start | bytes 196612
  12.4 74.3 %copy-start.4 = (bf16[256,256]{1,0:T(8,128)(2,1)S(1)}, bf16[256,256]{1,0:T(8,128)(2,1)}, u32[]{:S(2)}) copy-start(bf16[256,256]{1,0:T(8,128)(2,1)} %param.18) | copy-start | bytes 393220
  12.4 75.3 %copy-start.5 = (bf16[256,256]{1,0:T(8,128)(2,1)S(1)}, bf16[256,256]{1,0:T(8,128)(2,1)}, u32[]{:S(2)}) copy-start(bf16[256,256]{1,0:T(8,128)(2,1)} %param.16) | copy-start | bytes 393220
  12.4 75.4 %copy-start.7 = (bf16[256,256]{1,0:T(8,128)(2,1)S(1)}, bf16[256,256]{1,0:T(8,128)(2,1)}, u32[]{:S(2)}) copy-start(bf16[256,256]{1,0:T(8,128)(2,1)} %param.19) | copy-start | bytes 393220
  12.4 75.8 %copy-start.8 = (bf16[1,128,256]{2,1,0:T(8,128)(2,1)S(1)}, bf16[1,128,256]{2,1,0:T(8,128)(2,1)}, u32[]{:S(2)}) copy-start(bf16[1,128,256]{2,1,0:T(8,128)(2,1)} %param.15) | copy-start | bytes 196612
  78.5 124.8 %all-to-all-start = ((bf16[8,4096,128]{2,0,1:T(8,128)(2,1)}), bf16[8,4096,128]{2,0,1:T(8,128)(2,1)}, u32[]{:S(2)}, u32[]{:S(2)}) async-start(bf16[8,4096,128]{2,0,1:T(8,128)(2,1)} %all-gather.6.cloned.1.call-done), calls=%async_computation | async-start | bytes 16777216 | tf_op jit(solution)/shard_map/all_to_all | solution.py:152
  85.6 195.4 %all-gather.4.cloned.1.call-start = ((), (), s32[]{:S(2)}) async-start(), calls=%async_computation.5 | async-start | bytes 2162688 | tf_op jit(solution)/shard_map/all_gather | solution.py:148
  86.6 318.0 %all-gather.8.cloned.1.call-start = ((), (), s32[]{:S(2)}) async-start(), calls=%async_computation.7 | async-start | bytes 2162688 | tf_op jit(solution)/shard_map/all_gather | solution.py:149
  87.6 663.4 %reduce-scatter.10.cloned.1.call-start = ((), (), s32[]{:S(2)}) async-start(), calls=%async_computation.9 | async-start | bytes 2162688
  555.5 6.0 copy-start.2
  555.5 106.8 %all-to-all-start.1 = ((bf16[8,128,4096]{1,0,2:T(8,128)(2,1)}), bf16[8,128,4096]{1,0,2:T(8,128)(2,1)}, u32[]{:S(2)}, u32[]{:S(2)}) async-start(bf16[8,128,4096]{1,0,2:T(8,128)(2,1)} %copy.87), calls=%async_computation.1 | async-start | bytes 16777216 | tf_op jit(solution)/shard_map/all_to_all | solution.py:164
  561.4 347.7 %reduce-scatter.12.cloned.1.call-start = ((), (), s32[]{:S(2)}) async-start(), calls=%async_computation.10 | async-start | bytes 2162688
  577.8 432.8 %reduce-scatter.8.cloned.1.call-start = ((), (), s32[]{:S(2)}) async-start(), calls=%async_computation.8 | async-start | bytes 10485760 | tf_op jit(solution)/shard_map/reduce_scatter | solution.py:165
  910.6 104.0 %copy-start.1 = (bf16[256,256]{1,0:T(8,128)(2,1)S(1)}, bf16[256,256]{1,0:T(8,128)(2,1)}, u32[]{:S(2)}) copy-start(bf16[256,256]{1,0:T(8,128)(2,1)} %param.20) | copy-start | bytes 393220
Sparse Core Ops, SparseCore 0:
  12.5 65.9 all-gather.5
Sparse Core Ops, SparseCore 1:
  88.2 192.7 all-gather.3
  283.0 121.5 all-gather.7
  545.2 205.8 reduce-scatter.9
  753.5 155.5 reduce-scatter.11
  911.8 98.8 reduce-scatter.7
where the time goes:
time: 1030 us; the launch traced here: 1020 us
  waiting for transfers between devices  747 us (73%)
  matrix products  104 us (10%)
  local copies, waits for them, and re-layouts  88.8 us (9%)
  loops' own time  47.3 us (5%)
  between operations  16 us (2%)
  starting transfers between devices  13.3 us (1%)
    unnamed x8, waiting for transfers between devices  233 us
    all_to_all x1, waiting for transfers between devices, on_device(): lax.all_to_all(bias_cols, 'res', split_axis=1, concat_axis=2, tiled=True)  115 us
    reduce_scatter x1, waiting for transfers between devices, on_device(): lax.psum_scatter(moved_rows.astype(jnp.float32).astype(jnp.bfloat16), 'se...  99.2 us
    all_to_all x1, waiting for transfers between devices, on_device(): lax.all_to_all(bias_part, 'res', split_axis=2, concat_axis=1, tiled=True)  84.4 us
    all_gather x1, waiting for transfers between devices, on_device(): lax.all_gather(local_value_rows, 'res', axis=1, tiled=True)  83.3 us
    all_gather x1, waiting for transfers between devices, on_device(): bias_cols = lax.all_gather(residue_pair_bias, 'seq', axis=1, tiled=True)  66 us
    all_gather x1, waiting for transfers between devices, on_device(): lax.all_gather(local_key_rows, 'res', axis=1, tiled=True)  65.4 us
    dot_general x16, matrix products, block_scores(): jnp.einsum('bihd,bjhd->bhij', query_vectors, key_block, preferred_element...  34.6 us
  transfers between devices with their start and end apart: 8, of which 8 were waited for; matrix products, arithmetic and copies ran while one was open for 8% of the time, Pallas kernels for 0%

commit v1 on v0

v1 whole, which is shorter than its diff:
```python
import functools

import jax
import jax.numpy as jnp
from jax import lax
from jax.experimental import pallas as pl
from jax.experimental.pallas import tpu as pltpu
from jax.sharding import PartitionSpec as P

HEADS = 8
HD = 32
WIDTH = 256
ROWS = 1024
KEYS = 128
SEQS = 4
RES = 32
BLK = 128
CH = 256
F32 = jnp.float32
BF16 = jnp.bfloat16


def dot(a, b, dims):
    return lax.dot_general(a, b, (dims, ((), ())), preferred_element_type=F32)


NN = ((1,), (0,))
NT = ((1,), (1,))
TN = ((0,), (0,))


def load_chunk(qa_ref, s, which, h, c):
    rows = pl.ds(pl.multiple_of(h * HD, HD), HD)
    parts = [qa_ref[s * 8 + c * 2 + u, which, rows, :] for u in range(2)]
    return jnp.concatenate(parts, axis=1)


def stats_kernel(qa_ref, kh_ref, vh_ref, bias_ref, m_ref, l_ref, d_ref):
    def body(step, carry):
        h, c = step // 4, step % 4
        cols = pl.ds(pl.multiple_of(c * CH, CH), CH)
        bias = bias_ref[h, :, cols].astype(F32)
        for s in range(SEQS):
            qt = load_chunk(qa_ref, s, 0, h, c)
            at = load_chunk(qa_ref, s, 1, h, c)
            sc = dot(kh_ref[s, h], qt, NN) + bias
            top = jnp.max(sc, axis=0, keepdims=True)
            e = jnp.exp(sc - top)
            dp = dot(vh_ref[s, h], at, NN)
            m_ref[s, pl.ds(h, 1), cols] = top
            l_ref[s, pl.ds(h, 1), cols] = jnp.sum(e, axis=0, keepdims=True)
            d_ref[s, pl.ds(h, 1), cols] = jnp.sum(e * dp, axis=0, keepdims=True)
        return carry

    lax.fori_loop(0, 32, body, 0)


def grad_kernel(qa_ref, kh_ref, vh_ref, kt_ref, vt_ref, bias_ref, lt_ref, d_ref,
                od_ref, dk_ref, dv_ref, db_ref):
    dk_ref[...] = jnp.zeros_like(dk_ref)
    dv_ref[...] = jnp.zeros_like(dv_ref)

    def body(step, carry):
        h, c = step // 4, step % 4
        cols = pl.ds(pl.multiple_of(c * CH, CH), CH)
        rows = pl.ds(pl.multiple_of(h * HD, HD), HD)
        bias = bias_ref[h, :, cols].astype(F32)
        total = None
        for s in range(SEQS):
            qt = load_chunk(qa_ref, s, 0, h, c)
            at = load_chunk(qa_ref, s, 1, h, c)
            sc = dot(kh_ref[s, h], qt, NN) + bias
            p = jnp.exp(sc - lt_ref[s, pl.ds(h, 1), cols])
            dp = dot(vh_ref[s, h], at, NN)
            ds = p * (dp - d_ref[s, pl.ds(h, 1), cols])
            total = ds if total is None else total + ds
            pb = p.astype(BF16)
            db = ds.astype(BF16)
            o = dot(vt_ref[s, rows, :], pb, NN).astype(BF16)
            dq = dot(kt_ref[s, rows, :], db, NN).astype(BF16)
            for u in range(2):
                od_ref[s * 8 + c * 2 + u, 0, rows, :] = o[:, u * BLK:(u + 1) * BLK]
                od_ref[s * 8 + c * 2 + u, 1, rows, :] = dq[:, u * BLK:(u + 1) * BLK]
            dk_ref[s, h] += dot(db, qt, NT)
            dv_ref[s, h] += dot(pb, at, NT)
        for u in range(2):
            out = pl.ds(pl.multiple_of(c * CH + u * BLK, BLK), BLK)
            db_ref[h, out, :] = total[:, u * BLK:(u + 1) * BLK].T
        return carry

    lax.fori_loop(0, 32, body, 0)


def vmem(n):
    return [pl.BlockSpec(memory_space=pltpu.VMEM)] * n


def on_device(x, g, wq, wk, wv, wg, wr, bias):
    x, g = x[0], g[0]
    scale = HD ** -0.5
    qt = (dot(wq, x, ((0,), (1,))) * scale).astype(BF16)
    k = dot(x, wk, NN).astype(BF16)
    v = dot(x, wv, NN).astype(BF16)
    gate = jax.nn.sigmoid(dot(wg, x, ((0,), (1,))))
    gg = dot(wr, g, NT)
    at = (gg * gate).astype(BF16)
    swap = [(s * RES + z * 8 + t, z * RES + s * 8 + t) for s in range(4) for z in range(4) for t in range(8)]
    qa = lax.ppermute(jnp.stack([qt, at]), ("seq", "res"), swap)
    qa = lax.all_gather(qa, "res", axis=0, tiled=False)
    kv = lax.all_gather(jnp.stack([k, v]), "seq", axis=0, tiled=False)
    heads = kv.reshape(SEQS, 2, KEYS, HEADS, HD).transpose(1, 0, 3, 2, 4)
    flat = kv.transpose(1, 0, 3, 2)
    bias_t = bias.transpose(0, 2, 1)

    stat = jax.ShapeDtypeStruct((SEQS, HEADS, ROWS), F32)
    params = pltpu.CompilerParams(vmem_limit_bytes=48 * 2 ** 20)
    m, l, d = pl.pallas_call(
        stats_kernel, out_shape=[stat] * 3, in_specs=vmem(4), out_specs=vmem(3),
        compiler_params=params,
    )(qa, heads[0], heads[1], bias_t)
    top = lax.pmax(m, "res")
    fix = jnp.exp(m - top)
    both = lax.psum(jnp.stack([l * fix, d * fix]), "res")
    total = top + jnp.log(both[0])
    row_dot = both[1] / both[0]

    od, dk, dv, db = pl.pallas_call(
        grad_kernel,
        out_shape=[
            jax.ShapeDtypeStruct((RES, 2, WIDTH, BLK), BF16),
            jax.ShapeDtypeStruct((SEQS, HEADS, KEYS, HD), F32),
            jax.ShapeDtypeStruct((SEQS, HEADS, KEYS, HD), F32),
            jax.ShapeDtypeStruct((HEADS, ROWS, KEYS), F32),
        ],
        in_specs=vmem(8), out_specs=vmem(4),
        compiler_params=params,
    )(qa, heads[0], heads[1], flat[0], flat[1], bias_t, total, row_dot)

    od = lax.psum_scatter(od, "res", scatter_dimension=0, tiled=False)
    od = lax.ppermute(od, ("seq", "res"), swap)
    dkv = jnp.stack([dk, dv], axis=1).transpose(0, 1, 3, 2, 4).reshape(SEQS, 2, KEYS, WIDTH)
    dkv = lax.psum_scatter(dkv.astype(BF16), "seq", scatter_dimension=0, tiled=False)
    out = od[0].astype(F32)
    dq = (od[1].astype(F32) * scale).astype(BF16)
    dl = (gg * out * gate * (1.0 - gate)).astype(BF16)
    hom = dot(dq, wq, ((0,), (1,))) + dot(dl, wg, ((0,), (1,)))
    hom = hom + dot(dkv[0], wk, NT) + dot(dkv[1], wv, NT)
    return hom.astype(BF16)[None], db


def solution(mesh):
    return jax.shard_map(
        on_device,
        mesh=mesh,
        in_specs=(
            P("seq", "res", None), P("seq", "res", None), P(), P(), P(), P(), P(),
            P(None, "seq", "res"),
        ),
        out_specs=(P("seq", "res", None), P(None, "seq", "res")),
        check_vma=False,
    )
```

time: 1030 us -> 1030 us (level)
  waiting for transfers between devices: 747 us -> 898 us
  matrix products: 104 us -> 7.69 us
  local copies, waits for them, and re-layouts: 88.8 us -> 18.5 us
  Pallas kernels: 0 us -> 53.3 us
  loops' own time: 47.3 us -> 0 us
  blocking collectives: 0 us -> 14.5 us
    psum x0 -> x1, waiting for transfers between devices: none -> 295 us  [on_device(): both = lax.psum(jnp.stack([l * fix, d * fix]), 'res')]
    pmax x0 -> x1, waiting for transfers between devices: none -> 284 us  [on_device(): top = lax.pmax(m, 'res')]
    unnamed x8 -> x5, waiting for transfers between devices: 233 us -> 0.08 us
    all_to_all x2 -> x0, waiting for transfers between devices: 199 us -> none  [the longest x1 115 us: on_device(): lax.all_to_all(bias_cols, 'res', split_axis=1, concat_axis=2, tiled=True)]
    dot_general x65 -> x9, matrix products: 104 us -> 7.69 us  [dot(): return lax.dot_general(a, b, (dims, ((), ())), preferred_element_type=F32)]
    all_gather x3 -> x1, waiting for transfers between devices: 215 us -> 119 us  [on_device(): qa = lax.all_gather(qa, 'res', axis=0, tiled=False)]
    reduce_scatter x1 -> x2, waiting for transfers between devices: 99.2 us -> 194 us  [the longest x1 160 us: on_device(): od = lax.psum_scatter(od, 'res', scatter_dimension=0, tiled=False)]
    pallas_call x0 -> x2, Pallas kernels: none -> 53.3 us  [the longest x1 39.4 us: on_device(): pl.pallas_call(grad_kernel, out_shape=[jax.ShapeDtypeStruct((RES, 2, WIDT...]
  transfers between devices with their start and end apart: 8 -> 7, of which waited for: 8 -> 7; matrix products, arithmetic and copies ran while one was open for 8% -> 2% of each run, Pallas kernels for 0% -> 0%
where the time goes in v1:
time: 1030 us
  waiting for transfers between devices  898 us (87%)
  Pallas kernels  53.3 us (5%)
  local copies, waits for them, and re-layouts  18.5 us (2%)
  starting transfers between devices  16.3 us (2%)
  blocking collectives  14.5 us (1%)
  between operations  14.1 us (1%)
    psum x1, waiting for transfers between devices, on_device(): both = lax.psum(jnp.stack([l * fix, d * fix]), 'res')  295 us
    pmax x1, waiting for transfers between devices, on_device(): top = lax.pmax(m, 'res')  284 us
    reduce_scatter x1, waiting for transfers between devices, on_device(): od = lax.psum_scatter(od, 'res', scatter_dimension=0, tiled=False)  160 us
    all_gather x1, waiting for transfers between devices, on_device(): qa = lax.all_gather(qa, 'res', axis=0, tiled=False)  119 us
    pallas_call x1, Pallas kernels, on_device(): pl.pallas_call(grad_kernel, out_shape=[jax.ShapeDtypeStruct((RES, 2, WIDT...  39.4 us
    reduce_scatter x1, waiting for transfers between devices, on_device(): lax.psum_scatter(dkv.astype(BF16), 'seq', scatter_dimension=0, tiled=False)  34 us
  transfers between devices with their start and end apart: 7, of which 7 were waited for; matrix products, arithmetic and copies ran while one was open for 2% of the time, Pallas kernels for 0%

profile of v1, /device:TPU:1, one launch (start us, length us, event | category | flops | bytes accessed | tf_op | source)
XLA Modules:
  0.0 1029.9 jit_solution(15940083605731586575)
XLA Ops:
  9.1 1.1 fusion.2
  10.3 1.1 fusion.19
  12.2 4.9 collective-permute-start
  17.1 2.6 collective-permute-done
  21.8 14.5 %all-gather.1 = bf16[8,128,256]{2,1,0:T(8,128)(2,1)S(1)} all-gather(bf16[2,128,256]{2,1,0:T(8,128)(2,1)S(1)} %pad_maximum_fusion.3), channel_id=3, replica_groups=mesh['seq'=4,'res'=32] {'seq'}, dimensions={0}, use_global_device_ids=true | all-gather | bytes 655360 | tf_op jit(solution)/shard_map/all_gather | solution.py:110
  37.1 1.7 copy.17
  38.8 2.9 copy.19
  41.7 3.5 slice_bitcast_fusion
  45.2 119.0 %all-gather.4.cloned.1.call-done = bf16[64,256,128]{2,1,0:T(8,128)(2,1)} async-done(((bf16[2,256,128]{2,1,0:T(8,128)(2,1)}), bf16[64,256,128]{2,1,0:T(8,128)(2,1)}) %all-gather.4.cloned.1.call-update) | async-done | bytes 4194320 | tf_op jit(solution)/shard_map/all_gather | solution.py:109
  164.2 1.2 copy-done.2
  165.4 13.9 %shard_map.95 = (f32[4,8,1024]{2,1,0:T(8,128)}, f32[4,8,1024]{2,1,0:T(8,128)S(1)}, f32[4,8,1024]{2,1,0:T(8,128)S(1)}) custom-call(bf16[32,2,256,128]{3,2,1,0:T(8,128)(2,1)} %bitcast.78, bf16[4,8,128,32]{3,2,1,0:T(8,128)(2,1)S(1)} %copy-done.2, bf16[4,8,128,32]{3,2,1,0:T(8,128)(2,1)S(1)} %get-tuple-element.16.vh_ref, bf16[8,128,1024]{2,1,0:T(8,128)(2,1)S(1)} %bitcast.76), custom_call_target="tpu_custom_call" | custom-call | tf_op jit(solution)/shard_map/pallas_call | solution.py:117
  179.4 283.9 %all-reduce.3.cloned.1.call-done = f32[4,8,1024]{2,1,0:T(8,128)} async-done(((f32[4,8,1024]{2,1,0:T(8,128)}), f32[4,8,1024]{2,1,0:T(8,128)}) %all-reduce.3.cloned.1.call-update) | async-done | bytes 131088 | tf_op jit(solution)/shard_map/pmax | solution.py:121
  465.2 1.3 copy.18
  466.5 295.0 %all-reduce.5.cloned.1.call-done = f32[2,4,8,1024]{3,2,1,0:T(8,128)} async-done(((f32[2,4,8,1024]{3,2,1,0:T(8,128)}), f32[2,4,8,1024]{3,2,1,0:T(8,128)}) %all-reduce.5.cloned.1.call-update) | async-done | bytes 262160 | tf_op jit(solution)/shard_map/psum | solution.py:123
  763.5 39.4 %shard_map.96 = (bf16[32,2,256,128]{3,2,1,0:T(8,128)(2,1)}, f32[4,8,128,32]{3,2,1,0:T(8,128)S(1)}, f32[4,8,128,32]{3,2,1,0:T(8,128)}, f32[8,1024,128]{2,1,0:T(8,128)}) custom-call(bf16[32,2,256,128]{3,2,1,0:T(8,128)(2,1)} %bitcast.79, bf16[4,8,128,32]{3,2,1,0:T(8,128)(2,1)S(1)} %copy-done.3, bf16[4,8,128,32]{3,2,1,0:T(8,128)(2,1)S(1)} %get-tuple-element.16.vh_ref, ...), custom_call_target="tpu_custom_call" | custom-call | tf_op jit(solution)/shard_map/pallas_call | solution.py:127
  802.9 1.4 copy-done.4
  804.3 1.5 copy-done.5
  805.8 3.0 convert_bitcast_fusion
  808.8 1.6 copy.21
  811.7 160.2 %reduce-scatter.3.cloned.1.call-done = bf16[1,2,256,128]{3,2,1,0:T(8,128)(2,1)} async-done(((bf16[32,2,256,128]{3,2,1,0:T(8,128)(2,1)}), bf16[1,2,256,128]{3,2,1,0:T(8,128)(2,1)}) %reduce-scatter.3.cloned.1.call-update) | async-done | bytes 131088 | tf_op jit(solution)/shard_map/reduce_scatter | solution.py:139
  971.9 11.1 %collective-permute-start.1 = (bf16[2,256,128]{2,1,0:T(8,128)(2,1)}, bf16[2,256,128]{2,1,0:T(8,128)(2,1)S(1)}, u32[]{:S(2)}, u32[]{:S(2)}) collective-permute-start(bf16[2,256,128]{2,1,0:T(8,128)(2,1)} %bitcast.85), channel_id=1, source_target_pairs={{0,0},{1,1},{2,2},{3,3},{4,4},{5,5},{6,6},{7,7},{8,32},{9,33},{10,... | collective-permute-start | bytes 393224 | tf_op jit(solution)/shard_map/ppermute | solution.py:140
  983.0 3.2 collective-permute-done.1
  986.7 34.0 %reduce-scatter.5.cloned.1.call-done = bf16[1,2,128,256]{2,3,1,0:T(8,128)(2,1)} async-done(((bf16[4,2,128,256]{2,3,1,0:T(8,128)(2,1)}), bf16[1,2,128,256]{2,3,1,0:T(8,128)(2,1)}) %reduce-scatter.5.cloned.1.call-update) | async-done | bytes 131088 | tf_op jit(solution)/shard_map/reduce_scatter | solution.py:142
  1021.7 1.7 fusion.7
  (60 shorter events, 12.0 us)
Async XLA Ops:
  7.2 0.9 copy-start
  7.2 14.4 %copy-start.9 = (bf16[1,128,256]{2,1,0:T(8,128)(2,1)S(1)}, bf16[1,128,256]{2,1,0:T(8,128)(2,1)}, u32[]{:S(2)}) copy-start(bf16[1,128,256]{2,1,0:T(8,128)(2,1)} %param.8) | copy-start | bytes 196612
  7.2 14.4 %copy-start.11 = (bf16[256,256]{1,0:T(8,128)(2,1)S(1)}, bf16[256,256]{1,0:T(8,128)(2,1)}, u32[]{:S(2)}) copy-start(bf16[256,256]{1,0:T(8,128)(2,1)} %param.12) | copy-start | bytes 393220
  7.2 157.0 %all-gather.4.cloned.1.call-start = ((), (), s32[]{:S(2)}) async-start(), calls=%async_computation.6 | async-start | bytes 4325376 | tf_op jit(solution)/shard_map/all_gather | solution.py:109
  10.3 1.8 copy-start.14
  11.4 0.7 copy-start.7
  12.2 7.6 collective-permute-start
  20.4 442.9 %all-reduce.3.cloned.1.call-start = ((), (), s32[]{:S(2)}) async-start(), calls=%async_computation.2 | async-start | bytes 262144 | tf_op jit(solution)/shard_map/pmax | solution.py:121
  36.3 0.8 copy-start.6
  41.7 122.5 %copy-start.1 = (bf16[8,1024,128]{1,2,0:T(8,128)(2,1)}, bf16[8,1024,128]{1,2,0:T(8,128)(2,1)S(1)}, u32[]{:S(2)}) copy-start(bf16[8,1024,128]{1,2,0:T(8,128)(2,1)S(1)} %copy.19) | copy-start | bytes 6291460
  164.2 1.2 copy-start.2
  179.4 582.2 %all-reduce.5.cloned.1.call-start = ((), (), s32[]{:S(2)}) async-start(), calls=%async_computation.3 | async-start | bytes 524288 | tf_op jit(solution)/shard_map/psum | solution.py:123
  463.3 300.2 %copy-start.3 = (bf16[4,8,128,32]{3,2,1,0:T(8,128)(2,1)S(1)}, bf16[4,8,128,32]{3,2,1,0:T(8,128)(2,1)}, u32[]{:S(2)}) copy-start(bf16[4,8,128,32]{3,2,1,0:T(8,128)(2,1)} %get-tuple-element.17.kh_ref) | copy-start | bytes 786436
  464.4 297.2 %copy-start.13 = (f32[4,8,1024]{2,1,0:T(8,128)S(1)}, f32[4,8,1024]{2,1,0:T(8,128)}, u32[]{:S(2)}) copy-start(f32[4,8,1024]{2,1,0:T(8,128)} %all-reduce.3.cloned.1.call-done) | copy-start | bytes 393220
  465.1 506.8 %reduce-scatter.3.cloned.1.call-start = ((), (), s32[]{:S(2)}) async-start(), calls=%async_computation.4 | async-start | bytes 4325376 | tf_op jit(solution)/shard_map/reduce_scatter | solution.py:139
  802.9 1.4 copy-start.4
  804.3 1.6 copy-start.5
  804.3 216.4 %reduce-scatter.5.cloned.1.call-start = ((), (), s32[]{:S(2)}) async-start(), calls=%async_computation.5 | async-start | bytes 655360 | tf_op jit(solution)/shard_map/reduce_scatter | solution.py:142
  808.8 177.6 %copy-start.8 = (f32[256,128]{1,0:T(8,128)S(1)}, f32[256,128]{1,0:T(8,128)}, u32[]{:S(2)}) copy-start(f32[256,128]{1,0:T(8,128)} %copy-done.7) | copy-start | bytes 393220
  808.8 177.7 %copy-start.15 = (f32[256,128]{1,0:T(8,128)S(1)}, f32[256,128]{1,0:T(8,128)}, u32[]{:S(2)}) copy-start(f32[256,128]{1,0:T(8,128)} %copy-done.14) | copy-start | bytes 393220
  808.8 177.7 %copy-start.17 = (bf16[256,256]{1,0:T(8,128)(2,1)S(1)}, bf16[256,256]{1,0:T(8,128)(2,1)}, u32[]{:S(2)}) copy-start(bf16[256,256]{1,0:T(8,128)(2,1)} %param.13) | copy-start | bytes 393220
  810.4 210.2 %copy-start.10 = (bf16[256,256]{1,0:T(8,128)(2,1)S(1)}, bf16[256,256]{1,0:T(8,128)(2,1)}, u32[]{:S(2)}) copy-start(bf16[256,256]{1,0:T(8,128)(2,1)} %param.11) | copy-start | bytes 393220
  810.4 211.3 %copy-start.12 = (bf16[256,256]{1,0:T(8,128)(2,1)S(1)}, bf16[256,256]{1,0:T(8,128)(2,1)}, u32[]{:S(2)}) copy-start(bf16[256,256]{1,0:T(8,128)(2,1)} %param.12) | copy-start | bytes 393220
  971.9 14.4 %collective-permute-start.1 = (bf16[2,256,128]{2,1,0:T(8,128)(2,1)}, bf16[2,256,128]{2,1,0:T(8,128)(2,1)S(1)}, u32[]{:S(2)}, u32[]{:S(2)}) collective-permute-start(bf16[2,256,128]{2,1,0:T(8,128)(2,1)} %bitcast.85), channel_id=1, source_target_pairs={{0,0},{1,1},{2,2},{3,3},{4,4},{5,5},{6,6},{7,7},{8,32},{9,33},{10,... | collective-permute-start | bytes 393224 | tf_op jit(solution)/shard_map/ppermute | solution.py:140
  (1 other events, 0.6 us)
Sparse Core Ops, SparseCore 0:
  20.5 143.6 all-gather.3
  179.5 283.7 all-reduce.2
  466.4 295.0 all-reduce.4
  804.4 167.4 reduce-scatter.2
  974.3 46.3 reduce-scatter.4

commit v2 on v1

v2 whole, which is shorter than its diff:
```python
import jax
import jax.numpy as jnp
from jax import lax
from jax.experimental import pallas as pl
from jax.experimental.pallas import tpu as pltpu
from jax.sharding import PartitionSpec as P

HEADS = 8
HD = 32
WIDTH = 256
ROWS = 1024
KEYS = 128
SEQS = 4
RES = 32
BLK = 128
CH = 256
CHUNKS = 4
F32 = jnp.float32
BF16 = jnp.bfloat16
MESH = pl.DeviceIdType.MESH
SCALE = HD ** -0.5

NN = ((1,), (0,))
NT = ((1,), (1,))
TN = ((0,), (0,))
TT = ((0,), (1,))


def dot(a, b, dims):
    return lax.dot_general(a, b, (dims, ((), ())), preferred_element_type=F32)


def loop(n, body):
    def step(i, carry):
        body(i)
        return carry
    lax.fori_loop(0, n, step, 0)


def block(i, n):
    return pl.ds(pl.multiple_of(i * n, n), n)


def kernel(
    x_ref, g_ref, wq_ref, wk_ref, wv_ref, wg_ref, wr_ref, bias_hbm,
    hom_ref, db_ref,
    bias, bias_t, mine, qa, kv, heads, gate, gated, stat, stat_in, norm, norm_in, od, od_in, dkv, dkv_out, dkv_in, total,
    bias_sem, qa_send, qa_recv, kv_send, kv_recv, st_send, st_recv, nm_send, nm_recv, od_send, od_recv, dk_send, dk_recv,
):
    a = lax.axis_index("seq")
    b = lax.axis_index("res")
    z, t = b // 8, b % 8
    cm = t // 2

    def remote(src, dst, send, recv, seq, res):
        return pltpu.make_async_remote_copy(
            src_ref=src, dst_ref=dst, send_sem=send, recv_sem=recv,
            device_id=(seq, res), device_id_type=MESH)

    def send_to(src, dst, send, recv, seq, res):
        here = jnp.logical_and(seq == a, res == b)

        @pl.when(here)
        def _():
            pltpu.make_async_copy(src, dst, recv).start()

        @pl.when(jnp.logical_not(here))
        def _():
            remote(src, dst, send, recv, seq, res).start()

    def sent(src, send, seq, res):
        here = jnp.logical_and(seq == a, res == b)

        @pl.when(jnp.logical_not(here))
        def _():
            pltpu.make_async_copy(src, src, send).wait()

    def arrived(dst, recv):
        pltpu.make_async_copy(dst, dst, recv).wait()

    def dest(i):
        c = lax.rem(cm + i // 8, CHUNKS)
        r = i % 8
        return lax.rem(z + r // 2, 4) * 8 + c * 2 + r % 2

    bias_copy = pltpu.make_async_copy(bias_hbm, bias, bias_sem)
    bias_copy.start()

    x = x_ref[...]
    mine[0] = (dot(wq_ref[...], x, TT) * SCALE).astype(BF16)
    open_gate = jax.nn.sigmoid(dot(wg_ref[...], x, TT))
    gg = dot(wr_ref[...], g_ref[...], NT)
    mine[1] = (gg * open_gate).astype(BF16)
    gate[...] = open_gate
    gated[...] = gg
    kv[a, 0] = dot(wk_ref[...], x, TT).astype(BF16)
    kv[a, 1] = dot(wv_ref[...], x, TT).astype(BF16)

    for i in range(1, 4):
        other = lax.rem(a + i, 4)
        remote(kv.at[a], kv.at[a], kv_send.at[i], kv_recv.at[a], other, b).start()

    loop(RES, lambda i: send_to(mine, qa.at[a * 8 + t], qa_send.at[i], qa_recv.at[a * 8 + t], z, dest(i)))

    bias_copy.wait()

    def turn(i):
        h, r = i // 8, block(i % 8, BLK)
        bias_t[h, :, r] = bias[h, r, :].astype(F32).T.astype(BF16)
    loop(64, turn)

    for i in range(1, 4):
        other = lax.rem(a + i, 4)
        arrived(kv.at[other], kv_recv.at[other])

    def split(i):
        s, w = i // 2, i % 2
        rows = kv[s, w].astype(F32).T.astype(BF16)
        for h in range(HEADS):
            heads[w, s, h] = rows[:, h * HD:(h + 1) * HD]
    loop(8, split)

    def chunk_of(i):
        return lax.rem(cm + CHUNKS - i, CHUNKS)

    def rows_of(ref, s, w, h, c):
        return jnp.concatenate([ref[s * 8 + c * 2 + u, w, block(h, HD), :] for u in range(2)], axis=1)

    def line_of(ref, s, row, c):
        return jnp.concatenate([ref[s * 8 + c * 2 + u, pl.ds(row, 1), :] for u in range(2)], axis=1)

    def stats_chunk(step):
        c = chunk_of(step)

        def wait(i):
            n = (i // 2) * 8 + c * 2 + i % 2
            arrived(qa.at[n], qa_recv.at[n])
        loop(8, wait)

        def head(h):
            add = bias_t[h, :, block(c, CH)].astype(F32)
            for s in range(SEQS):
                sc = dot(heads[0, s, h], rows_of(qa, s, 0, h, c), NN) + add
                top = jnp.max(sc, axis=0, keepdims=True)
                e = jnp.exp(sc - top)
                dp = dot(heads[1, s, h], rows_of(qa, s, 1, h, c), NN)
                el = jnp.sum(e, axis=0, keepdims=True)
                ed = jnp.sum(e * dp, axis=0, keepdims=True)
                for u in range(2):
                    cut = slice(u * BLK, (u + 1) * BLK)
                    n = s * 8 + c * 2 + u
                    stat[n, pl.ds(h, 1), :] = top[:, cut]
                    stat[n, pl.ds(8 + h, 1), :] = el[:, cut]
                    stat[n, pl.ds(16 + h, 1), :] = ed[:, cut]
        loop(HEADS, head)

        def ship(i):
            s, tt = i // 2, c * 2 + i % 2
            n = s * 8 + tt
            send_to(stat.at[n], stat_in.at[b], st_send.at[n], st_recv.at[b], s, a * 8 + tt)
        loop(8, ship)
    loop(CHUNKS, stats_chunk)

    loop(RES, lambda i: arrived(stat_in.at[i], st_recv.at[i]))
    top = stat_in[0, 0:8, :]
    for i in range(1, RES):
        top = jnp.maximum(top, stat_in[i, 0:8, :])
    el = jnp.zeros((8, BLK), F32)
    ed = jnp.zeros((8, BLK), F32)
    for i in range(RES):
        fix = jnp.exp(stat_in[i, 0:8, :] - top)
        el = el + stat_in[i, 8:16, :] * fix
        ed = ed + stat_in[i, 16:24, :] * fix
    norm[0:8, :] = top + jnp.log(el)
    norm[8:16, :] = ed / el
    loop(RES, lambda i: send_to(norm, norm_in.at[a * 8 + t], nm_send.at[i], nm_recv.at[a * 8 + t], z, dest(i)))

    dkv[...] = jnp.zeros_like(dkv)

    def grad_chunk(step):
        c = chunk_of(step)

        def wait(i):
            n = (i // 2) * 8 + c * 2 + i % 2
            arrived(norm_in.at[n], nm_recv.at[n])
        loop(8, wait)

        def head(h):
            hr = block(h, HD)
            add = bias_t[h, :, block(c, CH)].astype(F32)
            acc = None
            for s in range(SEQS):
                qt = rows_of(qa, s, 0, h, c)
                at = rows_of(qa, s, 1, h, c)
                p = jnp.exp(dot(heads[0, s, h], qt, NN) + add - line_of(norm_in, s, h, c))
                ds = p * (dot(heads[1, s, h], at, NN) - line_of(norm_in, s, 8 + h, c))
                acc = ds if acc is None else acc + ds
                pb = p.astype(BF16)
                sb = ds.astype(BF16)
                o = dot(kv[s, 1, hr, :], pb, NN).astype(BF16)
                dq = dot(kv[s, 0, hr, :], sb, NN).astype(BF16)
                for u in range(2):
                    n = s * 8 + c * 2 + u
                    od[n, 0, hr, :] = o[:, u * BLK:(u + 1) * BLK]
                    od[n, 1, hr, :] = dq[:, u * BLK:(u + 1) * BLK]
                dkv[s, 0, hr, :] += dot(qt, sb, NT)
                dkv[s, 1, hr, :] += dot(at, pb, NT)
            for u in range(2):
                db_ref[h, block(c * 2 + u, BLK), :] = acc[:, u * BLK:(u + 1) * BLK].T.astype(BF16)
        loop(HEADS, head)

        def ship(i):
            s, tt = i // 2, c * 2 + i % 2
            n = s * 8 + tt
            send_to(od.at[n], od_in.at[b], od_send.at[n], od_recv.at[b], s, a * 8 + tt)
        loop(8, ship)
    loop(CHUNKS, grad_chunk)

    dkv_out[...] = dkv[...].astype(BF16)
    for i in range(1, 4):
        other = lax.rem(a + i, 4)
        remote(dkv_out.at[other], dkv_in.at[a], dk_send.at[i], dk_recv.at[a], other, b).start()

    total[...] = jnp.zeros_like(total)

    def add_part(i):
        arrived(od_in.at[i], od_recv.at[i])
        total[...] += od_in[i].astype(F32)
    loop(RES, add_part)

    dkv_sum = dkv[a]
    for i in range(1, 4):
        other = lax.rem(a + i, 4)
        arrived(dkv_in.at[other], dk_recv.at[other])
        dkv_sum = dkv_sum + dkv_in[other].astype(F32)
    grads = dkv_sum.astype(BF16)
    open_gate = gate[...]
    dl = (gated[...] * total[0] * open_gate * (1.0 - open_gate)).astype(BF16)
    dq = (total[1] * SCALE).astype(BF16)
    hom = dot(dq, wq_ref[...], TT) + dot(dl, wg_ref[...], TT)
    hom = hom + dot(grads[0], wk_ref[...], TT) + dot(grads[1], wv_ref[...], TT)
    hom_ref[...] = hom.astype(BF16)

    for i in range(1, 4):
        other = lax.rem(a + i, 4)
        pltpu.make_async_copy(kv.at[a], kv.at[a], kv_send.at[i]).wait()
        pltpu.make_async_copy(dkv_out.at[other], dkv_out.at[other], dk_send.at[i]).wait()

    def finish(i):
        sent(mine, qa_send.at[i], z, dest(i))
        sent(norm, nm_send.at[i], z, dest(i))
        sent(stat.at[i], st_send.at[i], i // 8, a * 8 + i % 8)
        sent(od.at[i], od_send.at[i], i // 8, a * 8 + i % 8)
    loop(RES, finish)


def on_device(x, g, wq, wk, wv, wg, wr, bias):
    vm = pl.BlockSpec(memory_space=pltpu.VMEM)
    dma = pltpu.SemaphoreType.DMA
    hom, db = pl.pallas_call(
        kernel,
        out_shape=[
            jax.ShapeDtypeStruct((BLK, WIDTH), BF16),
            jax.ShapeDtypeStruct((HEADS, ROWS, KEYS), BF16),
        ],
        in_specs=[vm] * 7 + [pl.BlockSpec(memory_space=pl.ANY)],
        out_specs=[vm, vm],
        scratch_shapes=[
            pltpu.VMEM((HEADS, ROWS, KEYS), BF16),
            pltpu.VMEM((HEADS, KEYS, ROWS), BF16),
            pltpu.VMEM((2, WIDTH, BLK), BF16),
            pltpu.VMEM((RES, 2, WIDTH, BLK), BF16),
            pltpu.VMEM((SEQS, 2, WIDTH, KEYS), BF16),
            pltpu.VMEM((2, SEQS, HEADS, KEYS, HD), BF16),
            pltpu.VMEM((WIDTH, BLK), F32),
            pltpu.VMEM((WIDTH, BLK), F32),
            pltpu.VMEM((RES, 24, BLK), F32),
            pltpu.VMEM((RES, 24, BLK), F32),
            pltpu.VMEM((16, BLK), F32),
            pltpu.VMEM((RES, 16, BLK), F32),
            pltpu.VMEM((RES, 2, WIDTH, BLK), BF16),
            pltpu.VMEM((RES, 2, WIDTH, BLK), BF16),
            pltpu.VMEM((SEQS, 2, WIDTH, KEYS), F32),
            pltpu.VMEM((SEQS, 2, WIDTH, KEYS), BF16),
            pltpu.VMEM((SEQS, 2, WIDTH, KEYS), BF16),
            pltpu.VMEM((2, WIDTH, BLK), F32),
            dma(()),
            dma((RES,)), dma((RES,)),
            dma((SEQS,)), dma((SEQS,)),
            dma((RES,)), dma((RES,)),
            dma((RES,)), dma((RES,)),
            dma((RES,)), dma((RES,)),
            dma((SEQS,)), dma((SEQS,)),
        ],
        compiler_params=pltpu.CompilerParams(vmem_limit_bytes=56 * 2 ** 20, has_side_effects=True),
        cost_estimate=pl.CostEstimate(flops=3 * 10 ** 9, bytes_accessed=10 ** 7, transcendentals=8 * 10 ** 6),
    )(x[0], g[0], wq, wk, wv, wg, wr, bias)
    return hom[None], db.astype(F32)


def solution(mesh):
    return jax.shard_map(
        on_device,
        mesh=mesh,
        in_specs=(
            P("seq", "res", None), P("seq", "res", None), P(), P(), P(), P(), P(),
            P(None, "seq", "res"),
        ),
        out_specs=(P("seq", "res", None), P(None, "seq", "res")),
        check_vma=False,
    )
```

time: 1030 us -> 271 us (0.26)
  waiting for transfers between devices: 898 us -> 0 us
  Pallas kernels: 53.3 us -> 264 us
  local copies, waits for them, and re-layouts: 18.5 us -> 0.63 us
  starting transfers between devices: 16.3 us -> 0 us
  blocking collectives: 14.5 us -> 0 us
  between operations: 14.1 us -> 0.65 us
    psum x1 -> x0, waiting for transfers between devices: 295 us -> none  [on_device(): both = lax.psum(jnp.stack([l * fix, d * fix]), 'res')]
    pmax x1 -> x0, waiting for transfers between devices: 284 us -> none  [on_device(): top = lax.pmax(m, 'res')]
    pallas_call x2 -> x1, Pallas kernels: 53.3 us -> 264 us  [on_device(): pl.pallas_call(kernel, out_shape=[jax.ShapeDtypeStruct((BLK, WIDTH), BF16...]
    reduce_scatter x2 -> x0, waiting for transfers between devices: 194 us -> none  [the longest x1 160 us: on_device(): od = lax.psum_scatter(od, 'res', scatter_dimension=0, tiled=False)]
    all_gather x1 -> x0, waiting for transfers between devices: 119 us -> none  [on_device(): qa = lax.all_gather(qa, 'res', axis=0, tiled=False)]
    ppermute x2 -> x0, starting transfers between devices: 16.1 us -> none  [the longest x1 11.1 us: on_device(): od = lax.ppermute(od, ('seq', 'res'), swap)]
    all_gather x1 -> x0, blocking collectives: 14.5 us -> none  [on_device(): kv = lax.all_gather(jnp.stack([k, v]), 'seq', axis=0, tiled=False)]
  transfers between devices with their start and end apart: 7 -> 0, of which waited for: 7 -> 0; matrix products, arithmetic and copies ran while one was open for 2% -> 0% of each run, Pallas kernels for 0% -> 0%
where the time goes in v2:
time: 271 us; the launch traced here: 269 us
  Pallas kernels  264 us (97%)
  other arithmetic  3.91 us (1%)
    pallas_call x1, Pallas kernels, on_device(): pl.pallas_call(kernel, out_shape=[jax.ShapeDtypeStruct((BLK, WIDTH), BF16...  264 us

profile of v2, /device:TPU:1, one launch (start us, length us, event | category | flops | bytes accessed | tf_op | source)
XLA Modules:
  0.0 269.4 jit_solution(18104361739467139595)
XLA Ops:
  0.6 264.2 %shard_map.95 = (bf16[128,256]{1,0:T(8,128)(2,1)}, bf16[8,1024,128]{2,1,0:T(8,128)(2,1)}) custom-call(bf16[128,256]{1,0:T(8,128)(2,1)} %bitcast.4, bf16[128,256]{1,0:T(8,128)(2,1)} %bitcast.5, bf16[256,256]{1,0:T(8,128)(2,1)} %wq_ref.1, bf16[256,256]{1,0:T(8,128)(2,1)} %wk_ref.1, bf16[256,256]{1,0:T(8,128)(2,1)} %wv_ref.1, bf16[256,256]{1,0:T(8,128)(2,1)} %wg_ref.1, ...), custom_call_target="tpu_custom_call" | custom-call | flops 3000000000 | bytes 10000000 | tf_op jit(solution)/shard_map/pallas_call | solution.py:260
  264.8 0.0 copy-start
  264.8 3.9 %convert_element_type.3 = f32[8,1024,128]{2,1,0:T(8,128)} convert(bf16[8,1024,128]{2,1,0:T(8,128)(2,1)} %get-tuple-element.5) | non-fusion elementwise | flops 1048576 | bytes 6291456 | tf_op jit(solution)/shard_map/convert_element_type | solution.py:298
  268.7 0.0 copy-done
  268.7 0.6 copy.11
Async XLA Ops:
  264.8 3.9 %copy-start = (bf16[128,256]{1,0:T(8,128)(2,1)S(1)}, bf16[128,256]{1,0:T(8,128)(2,1)}, u32[]{:S(2)}) copy-start(bf16[128,256]{1,0:T(8,128)(2,1)} %get-tuple-element.4) | copy-start | bytes 196612

commit v3 on v1

v3 whole, which is shorter than its diff:
```python
import jax
import jax.numpy as jnp
from jax import lax
from jax.experimental import pallas as pl
from jax.experimental.pallas import tpu as pltpu
from jax.sharding import PartitionSpec as P

HEADS = 8
NH = 4
HD = 32
WIDTH = 256
HALF = 128
ROWS = 1024
KEYS = 128
SEQS = 4
BLK = 128
CH = 256
F32 = jnp.float32
BF16 = jnp.bfloat16
MESH = pl.DeviceIdType.MESH
SCALE = HD ** -0.5
ORDER = (0, 1, 3, 2)
BACK = (2, 3, 1, 0)

NN = ((1,), (0,))
NT = ((1,), (1,))
TT = ((0,), (1,))


def dot(a, b, dims):
    return lax.dot_general(a, b, (dims, ((), ())), preferred_element_type=F32)


def loop(n, body):
    def step(i, carry):
        body(i)
        return carry
    lax.fori_loop(0, n, step, 0)


def block(i, n):
    return pl.ds(pl.multiple_of(i * n, n), n)


def mod4(v):
    return lax.rem(v, 4)


def kernel(
    x_ref, g_ref, wq_ref, wk_ref, wv_ref, wg_ref, wr_ref, bias_hbm,
    hom_ref, db_hbm,
    bias_in, bias_t, mine, kvm, qa, kv, heads, gate, gated, kept, kept_pg,
    stat, stat_in, norm, norm_in, part_o, part_q, in_o, in_q, mid_o, mid_q, mid_o_in, mid_q_in,
    fin_out, fin, dkv, dkv_out, dkv_in, db_t,
    bl_sem, bs_sem, br_sem, s0_send, qa_send, qa_recv, kv_send, kv_recv, st_send, st_recv, nm_send, nm_recv,
    o1_send, o1_recv, q1_send, q1_recv, o2_send, o2_recv, q2_send, q2_recv, fin_send, fin_recv, dk_send, dk_recv,
    dl_sem, ds_sem, dr_sem,
):
    a = lax.axis_index("seq")
    b = lax.axis_index("res")
    z, xl, y = b // 8, (b // 4) % 2, b % 4
    px = 1 - xl

    def at(zz, xx, yy):
        return zz * 8 + xx * 4 + yy

    def remote(src, dst, send, recv, seq, res):
        return pltpu.make_async_remote_copy(
            src_ref=src, dst_ref=dst, send_sem=send, recv_sem=recv,
            device_id=(seq, res), device_id_type=MESH)

    def push(src, dst, send, recv, seq, res):
        here = jnp.logical_and(seq == a, res == b)

        @pl.when(here)
        def _():
            pltpu.make_async_copy(src, dst, recv).start()

        @pl.when(jnp.logical_not(here))
        def _():
            remote(src, dst, send, recv, seq, res).start()

    def pushed(src, send, seq, res):
        here = jnp.logical_and(seq == a, res == b)

        @pl.when(jnp.logical_not(here))
        def _():
            pltpu.make_async_copy(src, src, send).wait()

    def wait(ref, sem):
        pltpu.make_async_copy(ref, ref, sem).wait()

    barrier = pltpu.get_barrier_semaphore()

    def greet(seq, res):
        @pl.when(jnp.logical_not(jnp.logical_and(seq == a, res == b)))
        def _():
            pl.semaphore_signal(barrier, inc=1, device_id=(seq, res), device_id_type=MESH)

    for h in range(2):
        greet(z, at(a, h, y))
        for s in range(SEQS):
            greet(s, at(z, h, y))
    for zz in range(4):
        for yy in range(4):
            greet(a, at(zz, xl, yy))

    own_bias = pltpu.make_async_copy(bias_hbm.at[pl.ds(xl * NH, NH)], bias_in.at[xl], bl_sem)
    own_bias.start()

    x = x_ref[...]
    qt = (dot(wq_ref[...], x, TT) * SCALE).astype(BF16)
    open_gate = jax.nn.sigmoid(dot(wg_ref[...], x, TT))
    gg = dot(wr_ref[...], g_ref[...], NT)
    gt = (gg * open_gate).astype(BF16)
    gate[...] = open_gate
    gated[...] = gg
    kt = dot(wk_ref[...], x, TT).astype(BF16)
    vt = dot(wv_ref[...], x, TT).astype(BF16)
    for h in range(2):
        cut = slice(h * HALF, (h + 1) * HALF)
        mine[h, 0] = qt[cut]
        mine[h, 1] = gt[cut]
        kvm[h, 0] = kt[cut]
        kvm[h, 1] = vt[cut]

    pl.semaphore_wait(barrier, jnp.where(a == z, 23, 24))

    slot = (a * 4 + y) * 2 + xl
    for h in range(2):
        push(mine.at[h], qa.at[slot], s0_send.at[h], qa_recv.at[slot], z, at(a, h, y))
    for i in range(4):
        s = mod4(a + i)
        for h in range(2):
            push(kvm.at[h], kv.at[a * 2 + xl], kv_send.at[s * 2 + h], kv_recv.at[a * 2 + xl], s, at(z, h, y))

    def bias_piece(n):
        rows = block(n, BLK)
        return remote(
            bias_hbm.at[pl.ds(px * NH, NH), rows, :], bias_in.at[xl, :, rows, :],
            bs_sem.at[n], br_sem.at[n], a, at(z, px, y))

    def piece(z0, y0, xs):
        return (z0 * 4 + y0) * 2 + xs

    def spread(n, k, zz, yy):
        remote(qa.at[n], qa.at[n], qa_send.at[k], qa_recv.at[n], a, at(zz, xl, yy)).start()

    home = [piece(z, y, 0), piece(z, y, 1)]
    wait(qa.at[home[0]], qa_recv.at[home[0]])
    for d in (3, 1, 2):
        spread(home[0], d - 1, z, mod4(y + d))
    wait(qa.at[home[1]], qa_recv.at[home[1]])
    for d in (3, 1, 2):
        spread(home[1], 2 + d, mod4(z + d), y)
    for d in (1, 3, 2):
        spread(home[0], 5 + d, mod4(z + d), y)
    for d in (3, 1, 2):
        spread(home[1], 17 + d, z, mod4(y + d))
    for i in ORDER:
        for xs in range(2):
            bias_piece(xs * 4 + mod4(y + i)).start()

    def turn(k, h, n):
        y0, xs = n % 4, n // 4
        tile = bias_in[k, h, block(n, BLK), :]
        bias_t[h, block(k, KEYS), block(y0 * 2 + xs, BLK)] = tile.astype(F32).T.astype(BF16)

    own_bias.wait()
    loop(32, lambda i: turn(xl, i // 8, i % 8))

    for j in (1, 3, 2):
        n = piece(z, mod4(y + j), 0)
        wait(qa.at[n], qa_recv.at[n])
        for d in (1, 3, 2):
            spread(n, 5 + 3 * j + d, mod4(z + d), y)
        n = piece(mod4(z + j), y, 1)
        wait(qa.at[n], qa_recv.at[n])
        for d in (3, 1, 2):
            spread(n, 17 + 3 * j + d, z, mod4(y + d))

    for i in range(8):
        wait(kv.at[i], kv_recv.at[i])

    def split(i):
        s, k, w = i // 4, (i // 2) % 2, i % 2
        rows = kv[s * 2 + k, w].astype(F32).T.astype(BF16)
        for h in range(NH):
            heads[w, s, h, block(k, KEYS), :] = rows[:, h * HD:(h + 1) * HD]
    loop(16, split)

    def rows_of(s, w, h, y0):
        return jnp.concatenate([qa[piece(s, y0, xs), w, block(h, HD), :] for xs in range(2)], axis=1)

    for i in ORDER:
        y0 = mod4(y + i)
        cols = block(y0, CH)
        for zz in range(4):
            for xs in range(2):
                n = piece(zz, y0, xs)
                known = [jnp.logical_and(zz == z, y0 == y)]
                known.append(jnp.logical_and(xs == 0, zz == z))
                known.append(jnp.logical_and(xs == 1, y0 == y))

                @pl.when(jnp.logical_not(jnp.logical_or(known[0], jnp.logical_or(known[1], known[2]))))
                def _():
                    wait(qa.at[n], qa_recv.at[n])
        for xs in range(2):
            bias_piece(xs * 4 + y0).wait_recv()
        loop(8, lambda j: turn(px, j // 2, (j % 2) * 4 + y0))

        def stats(h):
            add = bias_t[h, :, cols].astype(F32)
            for s in range(SEQS):
                sc = dot(heads[0, s, h], rows_of(s, 0, h, y0), NN) + add
                top = jnp.max(sc, axis=0, keepdims=True)
                e = jnp.exp(sc - top)
                pg = dot(heads[1, s, h], rows_of(s, 1, h, y0), NN)
                n = s * 4 + y0
                stat[n, pl.ds(h, 1), :] = top
                stat[n, pl.ds(4 + h, 1), :] = jnp.sum(e, axis=0, keepdims=True)
                stat[n, pl.ds(8 + h, 1), :] = jnp.sum(e * pg, axis=0, keepdims=True)
                kept[s, h, :, cols] = e
                kept_pg[s, h, :, cols] = pg
        loop(NH, stats)

        for s in range(SEQS):
            n = s * 4 + y0
            push(stat.at[n], stat_in.at[z * 4 + y], st_send.at[n], st_recv.at[z * 4 + y], a, at(s, xl, y0))

    for i in range(16):
        wait(stat_in.at[i], st_recv.at[i])
    top = stat_in[0, 0:4, :]
    for i in range(1, 16):
        top = jnp.maximum(top, stat_in[i, 0:4, :])
    el = jnp.zeros((4, CH), F32)
    ed = jnp.zeros((4, CH), F32)
    for i in range(16):
        fix = jnp.exp(stat_in[i, 0:4, :] - top)
        el = el + stat_in[i, 4:8, :] * fix
        ed = ed + stat_in[i, 8:12, :] * fix
    norm[0:4, :] = top + jnp.log(el)
    norm[4:8, :] = ed / el
    for i in BACK:
        for j in range(4):
            zz, yy = mod4(z + j), mod4(y + 4 - i)
            push(norm, norm_in.at[z * 4 + y], nm_send.at[zz * 4 + yy], nm_recv.at[z * 4 + y], a, at(zz, xl, yy))

    dkv[...] = jnp.zeros_like(dkv)

    def db_own(n):
        rows = block(n, BLK)
        return pltpu.make_async_copy(
            db_t.at[xl, :, rows, :], db_hbm.at[pl.ds(xl * NH, NH), rows, :], dl_sem.at[n])

    def db_far(n):
        rows = block(n, BLK)
        return remote(
            db_t.at[px, :, rows, :], db_hbm.at[pl.ds(xl * NH, NH), rows, :],
            ds_sem.at[n], dr_sem.at[n], a, at(z, px, y))

    for i in BACK:
        y0 = mod4(y + i)
        cols = block(y0, CH)
        for s in range(SEQS):
            n = s * 4 + y0
            wait(norm_in.at[n], nm_recv.at[n])

        def grads(h):
            hr = block(h, HD)
            acc = None
            for s in range(SEQS):
                n = s * 4 + y0
                qh = rows_of(s, 0, h, y0)
                gh = rows_of(s, 1, h, y0)
                fix = jnp.exp(stat[n, pl.ds(h, 1), :] - norm_in[n, pl.ds(h, 1), :])
                p = kept[s, h, :, cols] * fix
                ds = p * (kept_pg[s, h, :, cols] - norm_in[n, pl.ds(4 + h, 1), :])
                acc = ds if acc is None else acc + ds
                pb = p.astype(BF16)
                sb = ds.astype(BF16)
                kh = jnp.concatenate([kv[s * 2 + k, 0, hr, :] for k in range(2)], axis=1)
                vh = jnp.concatenate([kv[s * 2 + k, 1, hr, :] for k in range(2)], axis=1)
                part_o[s, y0, hr, :] = dot(vh, pb, NN).astype(BF16)
                part_q[y0, s, hr, :] = dot(kh, sb, NN).astype(BF16)
                dkv[s, 0, h] += dot(sb, qh, NT)
                dkv[s, 1, h] += dot(pb, gh, NT)
            for k in range(2):
                for xs in range(2):
                    tile = acc[k * KEYS:(k + 1) * KEYS, xs * BLK:(xs + 1) * BLK]
                    db_t[k, h, block(xs * 4 + y0, BLK), :] = tile.T.astype(BF16)
        loop(NH, grads)

        for xs in range(2):
            db_far(xs * 4 + y0).start()
            db_own(xs * 4 + y0).start()
        for d in (2, 1, 3):
            zz = mod4(z + d)
            remote(part_o.at[zz, y0], in_o.at[d, y0], o1_send.at[d * 4 + i], o1_recv.at[d * 4 + y0], a, at(zz, xl, y)).start()
        if i > 0:
            remote(part_q.at[y0], in_q.at[i], q1_send.at[i], q1_recv.at[i], a, at(z, xl, y0)).start()

    for s in range(SEQS):
        for k in range(2):
            for w in range(2):
                tiles = [dkv[s, w, h, k * KEYS:(k + 1) * KEYS, :] for h in range(NH)]
                dkv_out[s * 2 + k, w] = jnp.concatenate(tiles, axis=1).astype(BF16)
    for i in range(4):
        s = mod4(a + i)
        for k in range(2):
            push(dkv_out.at[s * 2 + k], dkv_in.at[a * 2 + xl], dk_send.at[s * 2 + k], dk_recv.at[a * 2 + xl], s, at(z, k, y))

    for i in BACK:
        zz = mod4(z + i)
        if i == 2:
            for d in (1, 2, 3):
                wait(in_q.at[d], q1_recv.at[d])
        acc = part_q[y, zz].astype(F32)
        for d in (1, 2, 3):
            acc = acc + in_q[d, zz].astype(F32)
        if i > 0:
            mid_q[i] = acc.astype(BF16)
            remote(mid_q.at[i], mid_q_in.at[i], q2_send.at[i], q2_recv.at[i], a, at(zz, xl, y)).start()
        else:
            sum_q = acc
    for i in BACK:
        yy = mod4(y + i)
        acc = part_o[z, yy].astype(F32)
        for d in (1, 2, 3):
            wait(in_o.at[d, yy], o1_recv.at[d * 4 + yy])
            acc = acc + in_o[d, yy].astype(F32)
        if i > 0:
            mid_o[i] = acc.astype(BF16)
            remote(mid_o.at[i], mid_o_in.at[i], o2_send.at[i], o2_recv.at[i], a, at(z, xl, yy)).start()
        else:
            sum_o = acc
    for d in (1, 3, 2):
        wait(mid_q_in.at[d], q2_recv.at[d])
        sum_q = sum_q + mid_q_in[d].astype(F32)
    for d in (1, 3, 2):
        wait(mid_o_in.at[d], o2_recv.at[d])
        sum_o = sum_o + mid_o_in[d].astype(F32)
    for xs in range(2):
        cut = slice(xs * BLK, (xs + 1) * BLK)
        fin_out[xs, 0] = sum_o[:, cut].astype(BF16)
        fin_out[xs, 1] = sum_q[:, cut].astype(BF16)
        push(fin_out.at[xs], fin.at[xl], fin_send.at[xs], fin_recv.at[xl], z, at(a, xs, y))

    hom = jnp.zeros((BLK, WIDTH), F32)
    for i in range(8):
        wait(dkv_in.at[i], dk_recv.at[i])
    for h in range(2):
        cut = slice(h * HALF, (h + 1) * HALF)
        for w, ref in ((0, wk_ref), (1, wv_ref)):
            acc = dkv_in[h, w].astype(F32)
            for s in range(1, SEQS):
                acc = acc + dkv_in[s * 2 + h, w].astype(F32)
            hom = hom + dot(acc.astype(BF16), ref[:, cut], NT)
    for h in range(2):
        wait(fin.at[h], fin_recv.at[h])
        cut = slice(h * HALF, (h + 1) * HALF)
        og = gate[cut, :]
        dl = (gated[cut, :] * fin[h, 0].astype(F32) * og * (1.0 - og)).astype(BF16)
        dq = (fin[h, 1].astype(F32) * SCALE).astype(BF16)
        hom = hom + dot(dq, wq_ref[:, cut], TT) + dot(dl, wg_ref[:, cut], TT)
    hom_ref[...] = hom.astype(BF16)

    for h in range(2):
        pushed(mine.at[h], s0_send.at[h], z, at(a, h, y))
        pushed(fin_out.at[h], fin_send.at[h], z, at(a, h, y))
        for s in range(SEQS):
            pushed(kvm.at[h], kv_send.at[s * 2 + h], s, at(z, h, y))
            pushed(dkv_out.at[s * 2 + h], dk_send.at[s * 2 + h], s, at(z, h, y))
    for k in range(30):
        wait(qa.at[0], qa_send.at[k])
    for n in range(16):
        pushed(stat.at[n], st_send.at[n], a, at(n // 4, xl, n % 4))
        pushed(norm, nm_send.at[n], a, at(n // 4, xl, n % 4))
    for d in (1, 2, 3):
        for i in range(4):
            wait(part_o.at[0, 0], o1_send.at[d * 4 + i])
        wait(part_q.at[0], q1_send.at[d])
        wait(mid_o.at[d], o2_send.at[d])
        wait(mid_q.at[d], q2_send.at[d])
    for n in range(8):
        bias_piece(n).wait_send()
        db_own(n).wait()
        db_far(n).wait()


def on_device(x, g, wq, wk, wv, wg, wr, bias):
    vm = pl.BlockSpec(memory_space=pltpu.VMEM)
    hbm = pl.BlockSpec(memory_space=pl.ANY)
    dma = pltpu.SemaphoreType.DMA
    V = pltpu.VMEM
    hom, db = pl.pallas_call(
        kernel,
        out_shape=[
            jax.ShapeDtypeStruct((BLK, WIDTH), BF16),
            jax.ShapeDtypeStruct((HEADS, ROWS, KEYS), BF16),
        ],
        in_specs=[vm] * 7 + [hbm],
        out_specs=[vm, hbm],
        scratch_shapes=[
            V((2, NH, ROWS, KEYS), BF16),
            V((NH, 2 * KEYS, ROWS), BF16),
            V((2, 2, HALF, BLK), BF16),
            V((2, 2, HALF, BLK), BF16),
            V((32, 2, HALF, BLK), BF16),
            V((8, 2, HALF, KEYS), BF16),
            V((2, SEQS, NH, 2 * KEYS, HD), BF16),
            V((WIDTH, BLK), F32),
            V((WIDTH, BLK), F32),
            V((SEQS, NH, 2 * KEYS, ROWS), F32),
            V((SEQS, NH, 2 * KEYS, ROWS), F32),
            V((16, 16, CH), F32),
            V((16, 16, CH), F32),
            V((8, CH), F32),
            V((16, 8, CH), F32),
            V((4, 4, HALF, CH), BF16),
            V((4, 4, HALF, CH), BF16),
            V((4, 4, HALF, CH), BF16),
            V((4, 4, HALF, CH), BF16),
            V((4, HALF, CH), BF16),
            V((4, HALF, CH), BF16),
            V((4, HALF, CH), BF16),
            V((4, HALF, CH), BF16),
            V((2, 2, HALF, BLK), BF16),
            V((2, 2, HALF, BLK), BF16),
            V((SEQS, 2, NH, 2 * KEYS, HD), F32),
            V((8, 2, KEYS, HALF), BF16),
            V((8, 2, KEYS, HALF), BF16),
            V((2, NH, ROWS, KEYS), BF16),
            dma(()), dma((8,)), dma((8,)),
            dma((2,)), dma((30,)), dma((32,)),
            dma((8,)), dma((8,)),
            dma((16,)), dma((16,)),
            dma((16,)), dma((16,)),
            dma((16,)), dma((16,)),
            dma((4,)), dma((4,)),
            dma((4,)), dma((4,)),
            dma((4,)), dma((4,)),
            dma((2,)), dma((2,)),
            dma((8,)), dma((8,)),
            dma((8,)), dma((8,)), dma((8,)),
        ],
        compiler_params=pltpu.CompilerParams(
            vmem_limit_bytes=60 * 2 ** 20, has_side_effects=True, collective_id=0),
        cost_estimate=pl.CostEstimate(flops=3 * 10 ** 9, bytes_accessed=10 ** 7, transcendentals=8 * 10 ** 6),
    )(x[0], g[0], wq, wk, wv, wg, wr, bias)
    return hom[None], db.astype(F32)


def solution(mesh):
    return jax.shard_map(
        on_device,
        mesh=mesh,
        in_specs=(
            P("seq", "res", None), P("seq", "res", None), P(), P(), P(), P(), P(),
            P(None, "seq", "res"),
        ),
        out_specs=(P("seq", "res", None), P(None, "seq", "res")),
        check_vma=False,
    )
```

time: 1030 us -> 95 us (0.09)
  waiting for transfers between devices: 898 us -> 0 us
  Pallas kernels: 53.3 us -> 89.1 us
  local copies, waits for them, and re-layouts: 18.5 us -> 0.63 us
  starting transfers between devices: 16.3 us -> 0 us
  blocking collectives: 14.5 us -> 0 us
  between operations: 14.1 us -> 0.65 us
    psum x1 -> x0, waiting for transfers between devices: 295 us -> none  [on_device(): both = lax.psum(jnp.stack([l * fix, d * fix]), 'res')]
    pmax x1 -> x0, waiting for transfers between devices: 284 us -> none  [on_device(): top = lax.pmax(m, 'res')]
    reduce_scatter x2 -> x0, waiting for transfers between devices: 194 us -> none  [the longest x1 160 us: on_device(): od = lax.psum_scatter(od, 'res', scatter_dimension=0, tiled=False)]
    all_gather x1 -> x0, waiting for transfers between devices: 119 us -> none  [on_device(): qa = lax.all_gather(qa, 'res', axis=0, tiled=False)]
    pallas_call x2 -> x1, Pallas kernels: 53.3 us -> 89.1 us  [on_device(): pl.pallas_call(kernel, out_shape=[jax.ShapeDtypeStruct((BLK, WIDTH), BF16...]
    ppermute x2 -> x0, starting transfers between devices: 16.1 us -> none  [the longest x1 11.1 us: on_device(): od = lax.ppermute(od, ('seq', 'res'), swap)]
    all_gather x1 -> x0, blocking collectives: 14.5 us -> none  [on_device(): kv = lax.all_gather(jnp.stack([k, v]), 'seq', axis=0, tiled=False)]
  transfers between devices with their start and end apart: 7 -> 0, of which waited for: 7 -> 0; matrix products, arithmetic and copies ran while one was open for 2% -> 0% of each run, Pallas kernels for 0% -> 0%
where the time goes in v3:
time: 95 us; the launch traced here: 94.3 us
  Pallas kernels  89.1 us (94%)
  other arithmetic  3.91 us (4%)
    pallas_call x1, Pallas kernels, on_device(): pl.pallas_call(kernel, out_shape=[jax.ShapeDtypeStruct((BLK, WIDTH), BF16...  89.1 us
    convert_element_type x1, other arithmetic, on_device(): return (hom[None], db.astype(F32))  3.91 us

profile of v3, /device:TPU:1, one launch (start us, length us, event | category | flops | bytes accessed | tf_op | source)
XLA Modules:
  0.0 94.3 jit_solution(17190353536765064491)
XLA Ops:
  0.6 89.1 %shard_map.95 = (bf16[128,256]{1,0:T(8,128)(2,1)}, bf16[8,1024,128]{2,1,0:T(8,128)(2,1)}) custom-call(bf16[128,256]{1,0:T(8,128)(2,1)} %bitcast.4, bf16[128,256]{1,0:T(8,128)(2,1)} %bitcast.5, bf16[256,256]{1,0:T(8,128)(2,1)} %wq_ref.1, bf16[256,256]{1,0:T(8,128)(2,1)} %wk_ref.1, bf16[256,256]{1,0:T(8,128)(2,1)} %wv_ref.1, bf16[256,256]{1,0:T(8,128)(2,1)} %wg_ref.1, ...), custom_call_target="tpu_custom_call" | custom-call | flops 3000000000 | bytes 10000000 | tf_op jit(solution)/shard_map/pallas_call | solution.py:396
  89.8 0.0 copy-start
  89.8 3.9 %convert_element_type.3 = f32[8,1024,128]{2,1,0:T(8,128)} convert(bf16[8,1024,128]{2,1,0:T(8,128)(2,1)} %get-tuple-element.5) | non-fusion elementwise | flops 1048576 | bytes 6291456 | tf_op jit(solution)/shard_map/convert_element_type | solution.py:451
  93.7 0.0 copy-done
  93.7 0.6 copy.11
Async XLA Ops:
  89.8 3.9 %copy-start = (bf16[128,256]{1,0:T(8,128)(2,1)S(1)}, bf16[128,256]{1,0:T(8,128)(2,1)}, u32[]{:S(2)}) copy-start(bf16[128,256]{1,0:T(8,128)(2,1)} %get-tuple-element.4) | copy-start | bytes 196612

commit v4 on v3

v4 whole, which is shorter than its diff:
```python
import jax
import jax.numpy as jnp
from jax import lax
from jax.experimental import pallas as pl
from jax.experimental.pallas import tpu as pltpu
from jax.sharding import PartitionSpec as P

HEADS = 8
NH = 4
GROUPS = 2
GH = 2
GW = 64
HD = 32
WIDTH = 256
HALF = 128
ROWS = 1024
KEYS = 128
SEQS = 4
BLK = 128
CH = 256
F32 = jnp.float32
BF16 = jnp.bfloat16
MESH = pl.DeviceIdType.MESH
SCALE = HD ** -0.5
ORDER = (0, 1, 3, 2)
BACK = (2, 3, 1, 0)

NN = ((1,), (0,))
NT = ((1,), (1,))
TT = ((0,), (1,))


def dot(a, b, dims):
    return lax.dot_general(a, b, (dims, ((), ())), preferred_element_type=F32)


def loop(n, body):
    def step(i, carry):
        body(i)
        return carry
    lax.fori_loop(0, n, step, 0)


def block(i, n):
    return pl.ds(pl.multiple_of(i * n, n), n)


def mod4(v):
    return lax.rem(v, 4)


def kernel(
    x_ref, g_ref, wq_ref, wk_ref, wv_ref, wg_ref, wr_ref, bias_hbm,
    hom_ref, db_hbm,
    bias_in, bias_t, mine, kvm, qa, kv, heads, gate, gated, kept, kept_pg,
    stat, stat_in, norm, norm_in, part_o, part_q, in_o, in_q, mid_o, mid_q, mid_o_in, mid_q_in,
    fin_out, fin, dkv, dkv_out, dkv_mid, dkv_sum, dkv_in, db_t,
    bl_sem, bs_sem, br_sem, s0_send, qa_send, qa_recv, kv_send, kv_recv, kr_send, st_send, st_recv, nm_send, nm_recv,
    o1_send, o1_recv, q1_send, q1_recv, o2_send, o2_recv, q2_send, q2_recv, fin_send, fin_recv,
    dm_send, dm_recv, dk_send, dk_recv, dl_sem, ds_sem, dr_sem,
):
    a = lax.axis_index("seq")
    b = lax.axis_index("res")
    z, xl, y = b // 8, (b // 4) % 2, b % 4
    px = 1 - xl
    xh, co = a // 2, a % 2
    twin = a + 1 - 2 * co

    def at(zz, xx, yy):
        return zz * 8 + xx * 4 + yy

    def remote(src, dst, send, recv, seq, res):
        return pltpu.make_async_remote_copy(
            src_ref=src, dst_ref=dst, send_sem=send, recv_sem=recv,
            device_id=(seq, res), device_id_type=MESH)

    def push(src, dst, send, recv, seq, res):
        here = jnp.logical_and(seq == a, res == b)

        @pl.when(here)
        def _():
            pltpu.make_async_copy(src, dst, recv).start()

        @pl.when(jnp.logical_not(here))
        def _():
            remote(src, dst, send, recv, seq, res).start()

    def pushed(src, send, seq, res):
        here = jnp.logical_and(seq == a, res == b)

        @pl.when(jnp.logical_not(here))
        def _():
            pltpu.make_async_copy(src, src, send).wait()

    def wait(ref, sem):
        pltpu.make_async_copy(ref, ref, sem).wait()

    barrier = pltpu.get_barrier_semaphore()

    def greet(seq, res):
        @pl.when(jnp.logical_not(jnp.logical_and(seq == a, res == b)))
        def _():
            pl.semaphore_signal(barrier, inc=1, device_id=(seq, res), device_id_type=MESH)

    for h in range(2):
        greet(z, at(a, h, y))
        for s in range(2):
            greet(s * 2 + co, at(z, h, y))
    greet(twin, b)
    for zz in range(4):
        for yy in range(4):
            greet(a, at(zz, xl, yy))

    own_bias = pltpu.make_async_copy(bias_hbm.at[pl.ds(xl * NH, NH)], bias_in.at[xl], bl_sem)
    own_bias.start()

    x = x_ref[...]
    qt = (dot(wq_ref[...], x, TT) * SCALE).astype(BF16)
    open_gate = jax.nn.sigmoid(dot(wg_ref[...], x, TT))
    gg = dot(wr_ref[...], g_ref[...], NT)
    gt = (gg * open_gate).astype(BF16)
    gate[...] = open_gate
    gated[...] = gg
    kt = dot(wk_ref[...], x, TT).astype(BF16)
    vt = dot(wv_ref[...], x, TT).astype(BF16)
    for h in range(2):
        for g in range(GROUPS):
            cut = slice(h * HALF + g * GW, h * HALF + (g + 1) * GW)
            mine[h, g, 0] = qt[cut]
            mine[h, g, 1] = gt[cut]
        cut = slice(h * HALF, (h + 1) * HALF)
        kvm[h, 0] = kt[cut]
        kvm[h, 1] = vt[cut]

    pl.semaphore_wait(barrier, jnp.where(a == z, 20, 21))

    slot = (a * 4 + y) * 2 + xl
    for g in range(GROUPS):
        for h in range(2):
            push(mine.at[h, g], qa.at[slot, g], s0_send.at[g * 2 + h], qa_recv.at[g * 32 + slot], z, at(a, h, y))
    for i in range(2):
        s = lax.rem(xh + i, 2)
        for h in range(2):
            push(kvm.at[h], kv.at[a * 2 + xl], kv_send.at[s * 2 + h], kv_recv.at[a * 2 + xl], s * 2 + co, at(z, h, y))

    def bias_piece(g, n):
        rows = block(n, BLK)
        return remote(
            bias_hbm.at[pl.ds(px * NH + g * GH, GH), rows, :], bias_in.at[xl, pl.ds(g * GH, GH), rows, :],
            bs_sem.at[g * 8 + n], br_sem.at[g * 8 + n], a, at(z, px, y))

    def bias_send(g):
        for i in ORDER:
            for xs in range(2):
                bias_piece(g, xs * 4 + mod4(y + i)).start()

    def piece(z0, y0, xs):
        return (z0 * 4 + y0) * 2 + xs

    def landed(g, n):
        wait(qa.at[n, g], qa_recv.at[g * 32 + n])

    def spread(g, n, k, zz, yy):
        remote(qa.at[n, g], qa.at[n, g], qa_send.at[g * 30 + k], qa_recv.at[g * 32 + n], a, at(zz, xl, yy)).start()

    bias_send(0)
    home = [piece(z, y, 0), piece(z, y, 1)]
    for g in range(GROUPS):
        landed(g, home[0])
        for d in (3, 1, 2):
            spread(g, home[0], d - 1, z, mod4(y + d))
        landed(g, home[1])
        for d in (3, 1, 2):
            spread(g, home[1], 2 + d, mod4(z + d), y)
        for d in (1, 3, 2):
            spread(g, home[0], 5 + d, mod4(z + d), y)
        for d in (3, 1, 2):
            spread(g, home[1], 17 + d, z, mod4(y + d))
    bias_send(1)

    def turn(k, h, n):
        y0, xs = n % 4, n // 4
        tile = bias_in[k, h, block(n, BLK), :]
        bias_t[h, block(k, KEYS), block(y0 * 2 + xs, BLK)] = tile.astype(F32).T.astype(BF16)

    own_bias.wait()
    loop(32, lambda i: turn(xl, i // 8, i % 8))

    for i in range(2):
        for k in range(2):
            n = (i * 2 + co) * 2 + k
            wait(kv.at[n], kv_recv.at[n])
            remote(kv.at[n], kv.at[n], kr_send.at[i * 2 + k], kv_recv.at[n], twin, b).start()

    for g in range(GROUPS):
        for j in (1, 3, 2):
            n = piece(z, mod4(y + j), 0)
            landed(g, n)
            for d in (1, 3, 2):
                spread(g, n, 5 + 3 * j + d, mod4(z + d), y)
            n = piece(mod4(z + j), y, 1)
            landed(g, n)
            for d in (3, 1, 2):
                spread(g, n, 17 + 3 * j + d, z, mod4(y + d))

    for i in range(2):
        for k in range(2):
            n = (i * 2 + 1 - co) * 2 + k
            wait(kv.at[n], kv_recv.at[n])

    def split(i):
        s, k, w = i // 4, (i // 2) % 2, i % 2
        rows = kv[s * 2 + k, w].astype(F32).T.astype(BF16)
        for h in range(NH):
            heads[w, s, h, block(k, KEYS), :] = rows[:, h * HD:(h + 1) * HD]
    loop(16, split)

    def rows_of(s, w, g, hh, y0):
        return jnp.concatenate([qa[piece(s, y0, xs), g, w, block(hh, HD), :] for xs in range(2)], axis=1)

    def stats_group(g):
        for i in ORDER:
            y0 = mod4(y + i)
            cols = block(y0, CH)
            if i > 0:
                for d in (1, 2, 3):
                    landed(g, piece(mod4(z + d), y0, 0))
                for d in range(4):
                    landed(g, piece(mod4(z + d), y0, 1))
            else:
                for d in (1, 2, 3):
                    landed(g, piece(mod4(z + d), y0, 0))
            for xs in range(2):
                bias_piece(g, xs * 4 + y0).wait_recv()
            loop(2 * GH, lambda j: turn(px, g * GH + j // 2, (j % 2) * 4 + y0))

            def stats(hh):
                h = g * GH + hh
                add = bias_t[h, :, cols].astype(F32)
                for s in range(SEQS):
                    sc = dot(heads[0, s, h], rows_of(s, 0, g, hh, y0), NN) + add
                    top = jnp.max(sc, axis=0, keepdims=True)
                    e = jnp.exp(sc - top)
                    pg = dot(heads[1, s, h], rows_of(s, 1, g, hh, y0), NN)
                    n = s * 4 + y0
                    stat[g, n, pl.ds(hh, 1), :] = top
                    stat[g, n, pl.ds(2 + hh, 1), :] = jnp.sum(e, axis=0, keepdims=True)
                    stat[g, n, pl.ds(4 + hh, 1), :] = jnp.sum(e * pg, axis=0, keepdims=True)
                    kept[s, h, :, cols] = e
                    kept_pg[s, h, :, cols] = pg
            loop(GH, stats)

            for s in range(SEQS):
                n = s * 4 + y0
                push(stat.at[g, n], stat_in.at[g, z * 4 + y], st_send.at[g * 16 + n],
                     st_recv.at[g * 16 + z * 4 + y], a, at(s, xl, y0))

    def combine(g):
        for i in range(16):
            wait(stat_in.at[g, i], st_recv.at[g * 16 + i])
        top = stat_in[g, 0, 0:2, :]
        for i in range(1, 16):
            top = jnp.maximum(top, stat_in[g, i, 0:2, :])
        el = jnp.zeros((2, CH), F32)
        ed = jnp.zeros((2, CH), F32)
        for i in range(16):
            fix = jnp.exp(stat_in[g, i, 0:2, :] - top)
            el = el + stat_in[g, i, 2:4, :] * fix
            ed = ed + stat_in[g, i, 4:6, :] * fix
        norm[g, 0:2, :] = top + jnp.log(el)
        norm[g, 2:4, :] = ed / el
        for i in BACK:
            for j in range(4):
                zz, yy = mod4(z + j), mod4(y + 4 - i)
                push(norm.at[g], norm_in.at[g, z * 4 + y], nm_send.at[g * 16 + zz * 4 + yy],
                     nm_recv.at[g * 16 + z * 4 + y], a, at(zz, xl, yy))

    def db_own(g, n):
        rows = block(n, BLK)
        return pltpu.make_async_copy(
            db_t.at[xl, pl.ds(g * GH, GH), rows, :], db_hbm.at[pl.ds(xl * NH + g * GH, GH), rows, :], dl_sem.at[g * 8 + n])

    def db_far(g, n):
        rows = block(n, BLK)
        return remote(
            db_t.at[px, pl.ds(g * GH, GH), rows, :], db_hbm.at[pl.ds(xl * NH + g * GH, GH), rows, :],
            ds_sem.at[g * 8 + n], dr_sem.at[g * 8 + n], a, at(z, px, y))

    def grads_group(g):
        for i in BACK:
            y0 = mod4(y + i)
            cols = block(y0, CH)
            for s in range(SEQS):
                n = s * 4 + y0
                wait(norm_in.at[g, n], nm_recv.at[g * 16 + n])

            def grads(hh):
                h = g * GH + hh
                hr = block(h, HD)
                gr = block(hh, HD)
                acc = None
                for s in range(SEQS):
                    n = s * 4 + y0
                    qh = rows_of(s, 0, g, hh, y0)
                    gh = rows_of(s, 1, g, hh, y0)
                    fix = jnp.exp(stat[g, n, pl.ds(hh, 1), :] - norm_in[g, n, pl.ds(hh, 1), :])
                    p = kept[s, h, :, cols] * fix
                    ds = p * (kept_pg[s, h, :, cols] - norm_in[g, n, pl.ds(2 + hh, 1), :])
                    acc = ds if acc is None else acc + ds
                    pb = p.astype(BF16)
                    sb = ds.astype(BF16)
                    kh = jnp.concatenate([kv[s * 2 + k, 0, hr, :] for k in range(2)], axis=1)
                    vh = jnp.concatenate([kv[s * 2 + k, 1, hr, :] for k in range(2)], axis=1)
                    part_o[g, s, y0, gr, :] = dot(vh, pb, NN).astype(BF16)
                    part_q[y0, g, s, gr, :] = dot(kh, sb, NN).astype(BF16)
                    dkv[s, 0, h] += dot(sb, qh, NT)
                    dkv[s, 1, h] += dot(pb, gh, NT)
                for k in range(2):
                    for xs in range(2):
                        tile = acc[k * KEYS:(k + 1) * KEYS, xs * BLK:(xs + 1) * BLK]
                        db_t[k, h, block(xs * 4 + y0, BLK), :] = tile.T.astype(BF16)
            loop(GH, grads)

            for xs in range(2):
                db_far(g, xs * 4 + y0).start()
                db_own(g, xs * 4 + y0).start()
            for d in (2, 1, 3):
                zz = mod4(z + d)
                remote(part_o.at[g, zz, y0], in_o.at[g, d, y0], o1_send.at[g * 16 + d * 4 + i],
                       o1_recv.at[g * 16 + d * 4 + y0], a, at(zz, xl, y)).start()
            if i > 0:
                remote(part_q.at[y0, g], in_q.at[i, g], q1_send.at[g * 4 + i], q1_recv.at[g * 4 + i], a, at(z, xl, y0)).start()

        for s in range(SEQS):
            for k in range(2):
                tiles = [dkv[s, w, g * GH + hh, k * KEYS:(k + 1) * KEYS, :] for w in range(2) for hh in range(GH)]
                dkv_out[g, s * 2 + k] = jnp.concatenate(tiles, axis=1).astype(BF16)
        for i in range(2):
            for k in range(2):
                remote(dkv_out.at[g, (i * 2 + 1 - co) * 2 + k], dkv_mid.at[g, i * 2 + k],
                       dm_send.at[g * 4 + i * 2 + k], dm_recv.at[g * 4 + i * 2 + k], twin, b).start()

    def key_grads(g):
        for j in range(2):
            i = lax.rem(xh + 1 + j, 2)
            for k in range(2):
                n = i * 2 + k
                wait(dkv_mid.at[g, n], dm_recv.at[g * 4 + n])
                both = dkv_out[g, (i * 2 + co) * 2 + k].astype(F32) + dkv_mid[g, n].astype(F32)
                dkv_sum[g, n] = both.astype(BF16)
                push(dkv_sum.at[g, n], dkv_in.at[g, xh * 2 + xl], dk_send.at[g * 4 + n],
                     dk_recv.at[g * 4 + xh * 2 + xl], i * 2 + co, at(z, k, y))

    dkv[...] = jnp.zeros_like(dkv)
    stats_group(0)
    combine(0)
    stats_group(1)
    grads_group(0)
    combine(1)
    key_grads(0)
    grads_group(1)
    key_grads(1)

    for g in range(GROUPS):
        for d in (1, 2, 3):
            wait(in_q.at[d, g], q1_recv.at[g * 4 + d])
    for i in BACK:
        zz = mod4(z + i)
        accs = []
        for g in range(GROUPS):
            acc = part_q[y, g, zz].astype(F32)
            for d in (1, 2, 3):
                acc = acc + in_q[d, g, zz].astype(F32)
            accs.append(acc)
        acc = jnp.concatenate(accs, axis=0)
        if i > 0:
            mid_q[i] = acc.astype(BF16)
            remote(mid_q.at[i], mid_q_in.at[i], q2_send.at[i], q2_recv.at[i], a, at(zz, xl, y)).start()
        else:
            sum_q = acc
    for i in BACK:
        yy = mod4(y + i)
        accs = []
        for g in range(GROUPS):
            acc = part_o[g, z, yy].astype(F32)
            for d in (1, 2, 3):
                wait(in_o.at[g, d, yy], o1_recv.at[g * 16 + d * 4 + yy])
                acc = acc + in_o[g, d, yy].astype(F32)
            accs.append(acc)
        acc = jnp.concatenate(accs, axis=0)
        if i > 0:
            mid_o[i] = acc.astype(BF16)
            remote(mid_o.at[i], mid_o_in.at[i], o2_send.at[i], o2_recv.at[i], a, at(z, xl, yy)).start()
        else:
            sum_o = acc
    for d in (1, 3, 2):
        wait(mid_q_in.at[d], q2_recv.at[d])
        sum_q = sum_q + mid_q_in[d].astype(F32)
    for d in (1, 3, 2):
        wait(mid_o_in.at[d], o2_recv.at[d])
        sum_o = sum_o + mid_o_in[d].astype(F32)
    for xs in range(2):
        cut = slice(xs * BLK, (xs + 1) * BLK)
        fin_out[xs, 0] = sum_o[:, cut].astype(BF16)
        fin_out[xs, 1] = sum_q[:, cut].astype(BF16)
        push(fin_out.at[xs], fin.at[xl], fin_send.at[xs], fin_recv.at[xl], z, at(a, xs, y))

    hom = jnp.zeros((BLK, WIDTH), F32)
    for g in range(GROUPS):
        for i in range(4):
            wait(dkv_in.at[g, i], dk_recv.at[g * 4 + i])
        for h in range(2):
            acc = (dkv_in[g, h].astype(F32) + dkv_in[g, 2 + h].astype(F32)).astype(BF16)
            cut = slice(h * HALF + g * GW, h * HALF + (g + 1) * GW)
            hom = hom + dot(acc[:, :GW], wk_ref[:, cut], NT) + dot(acc[:, GW:], wv_ref[:, cut], NT)
    for h in range(2):
        wait(fin.at[h], fin_recv.at[h])
        cut = slice(h * HALF, (h + 1) * HALF)
        og = gate[cut, :]
        dl = (gated[cut, :] * fin[h, 0].astype(F32) * og * (1.0 - og)).astype(BF16)
        dq = (fin[h, 1].astype(F32) * SCALE).astype(BF16)
        hom = hom + dot(dq, wq_ref[:, cut], TT) + dot(dl, wg_ref[:, cut], TT)
    hom_ref[...] = hom.astype(BF16)

    for h in range(2):
        pushed(fin_out.at[h], fin_send.at[h], z, at(a, h, y))
        for s in range(2):
            pushed(kvm.at[h], kv_send.at[s * 2 + h], s * 2 + co, at(z, h, y))
            wait(kv.at[0], kr_send.at[s * 2 + h])
    for g in range(GROUPS):
        for h in range(2):
            pushed(mine.at[h, g], s0_send.at[g * 2 + h], z, at(a, h, y))
            for s in range(2):
                n = s * 2 + h
                wait(dkv_mid.at[g, n], dm_send.at[g * 4 + n])
                pushed(dkv_sum.at[g, n], dk_send.at[g * 4 + n], s * 2 + co, at(z, h, y))
        for k in range(30):
            wait(qa.at[0, g], qa_send.at[g * 30 + k])
        for n in range(16):
            pushed(stat.at[g, n], st_send.at[g * 16 + n], a, at(n // 4, xl, n % 4))
            pushed(norm.at[g], nm_send.at[g * 16 + n], a, at(n // 4, xl, n % 4))
        for d in (1, 2, 3):
            for i in range(4):
                wait(part_o.at[g, 0, 0], o1_send.at[g * 16 + d * 4 + i])
            wait(part_q.at[0, g], q1_send.at[g * 4 + d])
        for n in range(8):
            bias_piece(g, n).wait_send()
            db_own(g, n).wait()
            db_far(g, n).wait()
    for d in (1, 2, 3):
        wait(mid_o.at[d], o2_send.at[d])
        wait(mid_q.at[d], q2_send.at[d])


def on_device(x, g, wq, wk, wv, wg, wr, bias):
    vm = pl.BlockSpec(memory_space=pltpu.VMEM)
    hbm = pl.BlockSpec(memory_space=pl.ANY)
    dma = pltpu.SemaphoreType.DMA
    V = pltpu.VMEM
    hom, db = pl.pallas_call(
        kernel,
        out_shape=[
            jax.ShapeDtypeStruct((BLK, WIDTH), BF16),
            jax.ShapeDtypeStruct((HEADS, ROWS, KEYS), BF16),
        ],
        in_specs=[vm] * 7 + [hbm],
        out_specs=[vm, hbm],
        scratch_shapes=[
            V((2, NH, ROWS, KEYS), BF16),
            V((NH, 2 * KEYS, ROWS), BF16),
            V((2, GROUPS, 2, GW, BLK), BF16),
            V((2, 2, HALF, BLK), BF16),
            V((32, GROUPS, 2, GW, BLK), BF16),
            V((8, 2, HALF, KEYS), BF16),
            V((2, SEQS, NH, 2 * KEYS, HD), BF16),
            V((WIDTH, BLK), F32),
            V((WIDTH, BLK), F32),
            V((SEQS, NH, 2 * KEYS, ROWS), F32),
            V((SEQS, NH, 2 * KEYS, ROWS), F32),
            V((GROUPS, 16, 8, CH), F32),
            V((GROUPS, 16, 8, CH), F32),
            V((GROUPS, 8, CH), F32),
            V((GROUPS, 16, 8, CH), F32),
            V((GROUPS, 4, 4, GW, CH), BF16),
            V((4, GROUPS, 4, GW, CH), BF16),
            V((GROUPS, 4, 4, GW, CH), BF16),
            V((4, GROUPS, 4, GW, CH), BF16),
            V((4, HALF, CH), BF16),
            V((4, HALF, CH), BF16),
            V((4, HALF, CH), BF16),
            V((4, HALF, CH), BF16),
            V((2, 2, HALF, BLK), BF16),
            V((2, 2, HALF, BLK), BF16),
            V((SEQS, 2, NH, 2 * KEYS, HD), F32),
            V((GROUPS, 8, KEYS, HALF), BF16),
            V((GROUPS, 4, KEYS, HALF), BF16),
            V((GROUPS, 4, KEYS, HALF), BF16),
            V((GROUPS, 4, KEYS, HALF), BF16),
            V((2, NH, ROWS, KEYS), BF16),
            dma(()), dma((16,)), dma((16,)),
            dma((4,)), dma((60,)), dma((64,)),
            dma((4,)), dma((8,)), dma((4,)),
            dma((32,)), dma((32,)),
            dma((32,)), dma((32,)),
            dma((32,)), dma((32,)),
            dma((8,)), dma((8,)),
            dma((4,)), dma((4,)),
            dma((4,)), dma((4,)),
            dma((2,)), dma((2,)),
            dma((8,)), dma((8,)),
            dma((8,)), dma((8,)),
            dma((16,)), dma((16,)), dma((16,)),
        ],
        compiler_params=pltpu.CompilerParams(
            vmem_limit_bytes=60 * 2 ** 20, has_side_effects=True, collective_id=0),
        cost_estimate=pl.CostEstimate(flops=3 * 10 ** 9, bytes_accessed=10 ** 7, transcendentals=8 * 10 ** 6),
    )(x[0], g[0], wq, wk, wv, wg, wr, bias)
    return hom[None], db.astype(F32)


def solution(mesh):
    return jax.shard_map(
        on_device,
        mesh=mesh,
        in_specs=(
            P("seq", "res", None), P("seq", "res", None), P(), P(), P(), P(), P(),
            P(None, "seq", "res"),
        ),
        out_specs=(P("seq", "res", None), P(None, "seq", "res")),
        check_vma=False,
    )
```

time: 95 us -> 84.1 us (0.89)
  Pallas kernels: 89.1 us -> 77.7 us
    pallas_call x1, Pallas kernels: 89.1 us -> 77.7 us  [on_device(): pl.pallas_call(kernel, out_shape=[jax.ShapeDtypeStruct((BLK, WIDTH), BF16...]
where the time goes in v4:
time: 84.1 us; the launch traced here: 82.9 us
  Pallas kernels  77.7 us (92%)
  other arithmetic  3.91 us (5%)
    pallas_call x1, Pallas kernels, on_device(): pl.pallas_call(kernel, out_shape=[jax.ShapeDtypeStruct((BLK, WIDTH), BF16...  77.7 us
    convert_element_type x1, other arithmetic, on_device(): return (hom[None], db.astype(F32))  3.91 us

profile of v4, /device:TPU:1, one launch (start us, length us, event | category | flops | bytes accessed | tf_op | source)
XLA Modules:
  0.0 82.9 jit_solution(2312015542480158024)
XLA Ops:
  0.6 77.7 %shard_map.95 = (bf16[128,256]{1,0:T(8,128)(2,1)}, bf16[8,1024,128]{2,1,0:T(8,128)(2,1)}) custom-call(bf16[128,256]{1,0:T(8,128)(2,1)} %bitcast.4, bf16[128,256]{1,0:T(8,128)(2,1)} %bitcast.5, bf16[256,256]{1,0:T(8,128)(2,1)} %wq_ref.1, bf16[256,256]{1,0:T(8,128)(2,1)} %wk_ref.1, bf16[256,256]{1,0:T(8,128)(2,1)} %wv_ref.1, bf16[256,256]{1,0:T(8,128)(2,1)} %wg_ref.1, ...), custom_call_target="tpu_custom_call" | custom-call | flops 3000000000 | bytes 10000000 | tf_op jit(solution)/shard_map/pallas_call | solution.py:460
  78.3 0.0 copy-start
  78.3 3.9 %convert_element_type.3 = f32[8,1024,128]{2,1,0:T(8,128)} convert(bf16[8,1024,128]{2,1,0:T(8,128)(2,1)} %get-tuple-element.5) | non-fusion elementwise | flops 1048576 | bytes 6291456 | tf_op jit(solution)/shard_map/convert_element_type | solution.py:518
  82.2 0.0 copy-done
  82.2 0.6 copy.11
Async XLA Ops:
  78.3 3.9 %copy-start = (bf16[128,256]{1,0:T(8,128)(2,1)S(1)}, bf16[128,256]{1,0:T(8,128)(2,1)}, u32[]{:S(2)}) copy-start(bf16[128,256]{1,0:T(8,128)(2,1)} %get-tuple-element.4) | copy-start | bytes 196612

commit v5 on v4

--- a/solution.py
+++ b/solution.py
@@ -52,7 +52,7 @@
 def kernel(
     x_ref, g_ref, wq_ref, wk_ref, wv_ref, wg_ref, wr_ref, bias_hbm,
     hom_ref, db_hbm,
-    bias_in, bias_t, mine, kvm, qa, kv, heads, gate, gated, kept, kept_pg,
+    bias_in, eye, mine, kvm, qa, kv, heads, gate, gated, kept, kept_pg,
     stat, stat_in, norm, norm_in, part_o, part_q, in_o, in_q, mid_o, mid_q, mid_o_in, mid_q_in,
     fin_out, fin, dkv, dkv_out, dkv_mid, dkv_sum, dkv_in, db_t,
     bl_sem, bs_sem, br_sem, s0_send, qa_send, qa_recv, kv_send, kv_recv, kr_send, st_send, st_recv, nm_send, nm_recv,
@@ -113,6 +113,9 @@
 
     own_bias = pltpu.make_async_copy(bias_hbm.at[pl.ds(xl * NH, NH)], bias_in.at[xl], bl_sem)
     own_bias.start()
+
+    same = lax.broadcasted_iota(jnp.int32, (KEYS, KEYS), 0) == lax.broadcasted_iota(jnp.int32, (KEYS, KEYS), 1)
+    eye[...] = jnp.where(same, 1.0, 0.0).astype(BF16)
 
     x = x_ref[...]
     qt = (dot(wq_ref[...], x, TT) * SCALE).astype(BF16)
@@ -178,13 +181,7 @@
             spread(g, home[1], 17 + d, z, mod4(y + d))
     bias_send(1)
 
-    def turn(k, h, n):
-        y0, xs = n % 4, n // 4
-        tile = bias_in[k, h, block(n, BLK), :]
-        bias_t[h, block(k, KEYS), block(y0 * 2 + xs, BLK)] = tile.astype(F32).T.astype(BF16)
-
     own_bias.wait()
-    loop(32, lambda i: turn(xl, i // 8, i % 8))
 
     for i in range(2):
         for k in range(2):
@@ -218,7 +215,7 @@
     def rows_of(s, w, g, hh, y0):
         return jnp.concatenate([qa[piece(s, y0, xs), g, w, block(hh, HD), :] for xs in range(2)], axis=1)
 
-    def stats_group(g):
+    def stats_group(g, between):
         for i in ORDER:
             y0 = mod4(y + i)
             cols = block(y0, CH)
@@ -232,11 +229,12 @@
                     landed(g, piece(mod4(z + d), y0, 0))
             for xs in range(2):
                 bias_piece(g, xs * 4 + y0).wait_recv()
-            loop(2 * GH, lambda j: turn(px, g * GH + j // 2, (j % 2) * 4 + y0))
 
             def stats(hh):
                 h = g * GH + hh
-                add = bias_t[h, :, cols].astype(F32)
+                add = jnp.concatenate([
+                    jnp.concatenate([dot(eye[...], bias_in[k, h, block(xs * 4 + y0, BLK), :], NT) for xs in range(2)], axis=1)
+                    for k in range(2)], axis=0)
                 for s in range(SEQS):
                     sc = dot(heads[0, s, h], rows_of(s, 0, g, hh, y0), NN) + add
                     top = jnp.max(sc, axis=0, keepdims=True)
@@ -254,6 +252,8 @@
                 n = s * 4 + y0
                 push(stat.at[g, n], stat_in.at[g, z * 4 + y], st_send.at[g * 16 + n],
                      st_recv.at[g * 16 + z * 4 + y], a, at(s, xl, y0))
+            if i == 1:
+                between()
 
     def combine(g):
         for i in range(16):
@@ -352,9 +352,8 @@
                      dk_recv.at[g * 4 + xh * 2 + xl], i * 2 + co, at(z, k, y))
 
     dkv[...] = jnp.zeros_like(dkv)
-    stats_group(0)
-    combine(0)
-    stats_group(1)
+    stats_group(0, lambda: None)
+    stats_group(1, lambda: combine(0))
     grads_group(0)
     combine(1)
     key_grads(0)
@@ -467,7 +466,7 @@
         out_specs=[vm, hbm],
         scratch_shapes=[
             V((2, NH, ROWS, KEYS), BF16),
-            V((NH, 2 * KEYS, ROWS), BF16),
+            V((KEYS, KEYS), BF16),
             V((2, GROUPS, 2, GW, BLK), BF16),
             V((2, 2, HALF, BLK), BF16),
             V((32, GROUPS, 2, GW, BLK), BF16),

time: 84.1 us -> 80.9 us (0.962)
  Pallas kernels: 77.7 us -> 74.2 us
    pallas_call x1, Pallas kernels: 77.7 us -> 74.2 us  [on_device(): pl.pallas_call(kernel, out_shape=[jax.ShapeDtypeStruct((BLK, WIDTH), BF16...]
where the time goes in v5:
time: 80.9 us; the launch traced here: 79.4 us
  Pallas kernels  74.2 us (92%)
  other arithmetic  3.91 us (5%)
    pallas_call x1, Pallas kernels, on_device(): pl.pallas_call(kernel, out_shape=[jax.ShapeDtypeStruct((BLK, WIDTH), BF16...  74.2 us
    convert_element_type x1, other arithmetic, on_device(): return (hom[None], db.astype(F32))  3.91 us

profile of v5, /device:TPU:1, one launch (start us, length us, event | category | flops | bytes accessed | tf_op | source)
XLA Modules:
  0.0 79.4 jit_solution(9443427625772898377)
XLA Ops:
  0.6 74.2 %shard_map.95 = (bf16[128,256]{1,0:T(8,128)(2,1)}, bf16[8,1024,128]{2,1,0:T(8,128)(2,1)}) custom-call(bf16[128,256]{1,0:T(8,128)(2,1)} %bitcast.4, bf16[128,256]{1,0:T(8,128)(2,1)} %bitcast.5, bf16[256,256]{1,0:T(8,128)(2,1)} %wq_ref.1, bf16[256,256]{1,0:T(8,128)(2,1)} %wk_ref.1, bf16[256,256]{1,0:T(8,128)(2,1)} %wv_ref.1, bf16[256,256]{1,0:T(8,128)(2,1)} %wg_ref.1, ...), custom_call_target="tpu_custom_call" | custom-call | flops 3000000000 | bytes 10000000 | tf_op jit(solution)/shard_map/pallas_call | solution.py:459
  74.8 0.0 copy-start
  74.8 3.9 %convert_element_type.3 = f32[8,1024,128]{2,1,0:T(8,128)} convert(bf16[8,1024,128]{2,1,0:T(8,128)(2,1)} %get-tuple-element.5) | non-fusion elementwise | flops 1048576 | bytes 6291456 | tf_op jit(solution)/shard_map/convert_element_type | solution.py:517
  78.7 0.0 copy-done
  78.7 0.6 copy.11
Async XLA Ops:
  74.8 3.9 %copy-start = (bf16[128,256]{1,0:T(8,128)(2,1)S(1)}, bf16[128,256]{1,0:T(8,128)(2,1)}, u32[]{:S(2)}) copy-start(bf16[128,256]{1,0:T(8,128)(2,1)} %get-tuple-element.4) | copy-start | bytes 196612

commit v6 on v5

--- a/solution.py
+++ b/solution.py
@@ -135,6 +135,7 @@
         kvm[h, 0] = kt[cut]
         kvm[h, 1] = vt[cut]
 
+    dkv[...] = jnp.zeros_like(dkv)
     pl.semaphore_wait(barrier, jnp.where(a == z, 20, 21))
 
     slot = (a * 4 + y) * 2 + xl
@@ -246,7 +247,8 @@
                     stat[g, n, pl.ds(4 + hh, 1), :] = jnp.sum(e * pg, axis=0, keepdims=True)
                     kept[s, h, :, cols] = e
                     kept_pg[s, h, :, cols] = pg
-            loop(GH, stats)
+            for hh in range(GH):
+                stats(hh)
 
             for s in range(SEQS):
                 n = s * 4 + y0
@@ -319,7 +321,8 @@
                     for xs in range(2):
                         tile = acc[k * KEYS:(k + 1) * KEYS, xs * BLK:(xs + 1) * BLK]
                         db_t[k, h, block(xs * 4 + y0, BLK), :] = tile.T.astype(BF16)
-            loop(GH, grads)
+            for hh in range(GH):
+                grads(hh)
 
             for xs in range(2):
                 db_far(g, xs * 4 + y0).start()
@@ -351,7 +354,6 @@
                 push(dkv_sum.at[g, n], dkv_in.at[g, xh * 2 + xl], dk_send.at[g * 4 + n],
                      dk_recv.at[g * 4 + xh * 2 + xl], i * 2 + co, at(z, k, y))
 
-    dkv[...] = jnp.zeros_like(dkv)
     stats_group(0, lambda: None)
     stats_group(1, lambda: combine(0))
     grads_group(0)
@@ -392,6 +394,27 @@
             remote(mid_o.at[i], mid_o_in.at[i], o2_send.at[i], o2_recv.at[i], a, at(z, xl, yy)).start()
         else:
             sum_o = acc
+    for h in range(2):
+        for s in range(2):
+            pushed(kvm.at[h], kv_send.at[s * 2 + h], s * 2 + co, at(z, h, y))
+            wait(kv.at[0], kr_send.at[s * 2 + h])
+    for g in range(GROUPS):
+        for h in range(2):
+            pushed(mine.at[h, g], s0_send.at[g * 2 + h], z, at(a, h, y))
+            for s in range(2):
+                n = s * 2 + h
+                wait(dkv_mid.at[g, n], dm_send.at[g * 4 + n])
+        for k in range(30):
+            wait(qa.at[0, g], qa_send.at[g * 30 + k])
+        for n in range(16):
+            pushed(stat.at[g, n], st_send.at[g * 16 + n], a, at(n // 4, xl, n % 4))
+            pushed(norm.at[g], nm_send.at[g * 16 + n], a, at(n // 4, xl, n % 4))
+        for d in (1, 2, 3):
+            for i in range(4):
+                wait(part_o.at[g, 0, 0], o1_send.at[g * 16 + d * 4 + i])
+            wait(part_q.at[0, g], q1_send.at[g * 4 + d])
+        for n in range(8):
+            bias_piece(g, n).wait_send()
     for d in (1, 3, 2):
         wait(mid_q_in.at[d], q2_recv.at[d])
         sum_q = sum_q + mid_q_in[d].astype(F32)
@@ -424,26 +447,11 @@
     for h in range(2):
         pushed(fin_out.at[h], fin_send.at[h], z, at(a, h, y))
         for s in range(2):
-            pushed(kvm.at[h], kv_send.at[s * 2 + h], s * 2 + co, at(z, h, y))
-            wait(kv.at[0], kr_send.at[s * 2 + h])
-    for g in range(GROUPS):
-        for h in range(2):
-            pushed(mine.at[h, g], s0_send.at[g * 2 + h], z, at(a, h, y))
-            for s in range(2):
+            for g in range(GROUPS):
                 n = s * 2 + h
-                wait(dkv_mid.at[g, n], dm_send.at[g * 4 + n])
                 pushed(dkv_sum.at[g, n], dk_send.at[g * 4 + n], s * 2 + co, at(z, h, y))
-        for k in range(30):
-            wait(qa.at[0, g], qa_send.at[g * 30 + k])
-        for n in range(16):
-            pushed(stat.at[g, n], st_send.at[g * 16 + n], a, at(n // 4, xl, n % 4))
-            pushed(norm.at[g], nm_send.at[g * 16 + n], a, at(n // 4, xl, n % 4))
-        for d in (1, 2, 3):
-            for i in range(4):
-                wait(part_o.at[g, 0, 0], o1_send.at[g * 16 + d * 4 + i])
-            wait(part_q.at[0, g], q1_send.at[g * 4 + d])
+    for g in range(GROUPS):
         for n in range(8):
-            bias_piece(g, n).wait_send()
             db_own(g, n).wait()
             db_far(g, n).wait()
     for d in (1, 2, 3):

time: 80.9 us -> 78 us (0.964); the launches traced: 79.4 us -> 77.7 us
  Pallas kernels: 74.2 us -> 72.5 us
    pallas_call x1, Pallas kernels: 74.2 us -> 72.5 us  [on_device(): pl.pallas_call(kernel, out_shape=[jax.ShapeDtypeStruct((BLK, WIDTH), BF16...]
where the time goes in v6:
time: 78 us; the launch traced here: 77.7 us
  Pallas kernels  72.5 us (93%)
  other arithmetic  3.91 us (5%)
    pallas_call x1, Pallas kernels, on_device(): pl.pallas_call(kernel, out_shape=[jax.ShapeDtypeStruct((BLK, WIDTH), BF16...  72.5 us
    convert_element_type x1, other arithmetic, on_device(): return (hom[None], db.astype(F32))  3.91 us

profile of v6, /device:TPU:1, one launch (start us, length us, event | category | flops | bytes accessed | tf_op | source)
XLA Modules:
  0.0 77.7 jit_solution(6707638046424672026)
XLA Ops:
  0.6 72.5 %shard_map.95 = (bf16[128,256]{1,0:T(8,128)(2,1)}, bf16[8,1024,128]{2,1,0:T(8,128)(2,1)}) custom-call(bf16[128,256]{1,0:T(8,128)(2,1)} %bitcast.4, bf16[128,256]{1,0:T(8,128)(2,1)} %bitcast.5, bf16[256,256]{1,0:T(8,128)(2,1)} %wq_ref.1, bf16[256,256]{1,0:T(8,128)(2,1)} %wk_ref.1, bf16[256,256]{1,0:T(8,128)(2,1)} %wv_ref.1, bf16[256,256]{1,0:T(8,128)(2,1)} %wg_ref.1, ...), custom_call_target="tpu_custom_call" | custom-call | flops 3000000000 | bytes 10000000 | tf_op jit(solution)/shard_map/pallas_call | solution.py:467
  73.2 0.0 copy-start
  73.2 3.9 %convert_element_type.3 = f32[8,1024,128]{2,1,0:T(8,128)} convert(bf16[8,1024,128]{2,1,0:T(8,128)(2,1)} %get-tuple-element.5) | non-fusion elementwise | flops 1048576 | bytes 6291456 | tf_op jit(solution)/shard_map/convert_element_type | solution.py:525
  77.1 0.0 copy-done
  77.1 0.6 copy.11
Async XLA Ops:
  73.2 3.9 %copy-start = (bf16[128,256]{1,0:T(8,128)(2,1)S(1)}, bf16[128,256]{1,0:T(8,128)(2,1)}, u32[]{:S(2)}) copy-start(bf16[128,256]{1,0:T(8,128)(2,1)} %get-tuple-element.4) | copy-start | bytes 196612

commit v7 on v6

--- a/solution.py
+++ b/solution.py
@@ -135,7 +135,6 @@
         kvm[h, 0] = kt[cut]
         kvm[h, 1] = vt[cut]
 
-    dkv[...] = jnp.zeros_like(dkv)
     pl.semaphore_wait(barrier, jnp.where(a == z, 20, 21))
 
     slot = (a * 4 + y) * 2 + xl
@@ -315,8 +314,10 @@
                     vh = jnp.concatenate([kv[s * 2 + k, 1, hr, :] for k in range(2)], axis=1)
                     part_o[g, s, y0, gr, :] = dot(vh, pb, NN).astype(BF16)
                     part_q[y0, g, s, gr, :] = dot(kh, sb, NN).astype(BF16)
-                    dkv[s, 0, h] += dot(sb, qh, NT)
-                    dkv[s, 1, h] += dot(pb, gh, NT)
+                    dk = dot(sb, qh, NT)
+                    dv = dot(pb, gh, NT)
+                    dkv[s, 0, h] = dk if i == BACK[0] else dkv[s, 0, h] + dk
+                    dkv[s, 1, h] = dv if i == BACK[0] else dkv[s, 1, h] + dv
                 for k in range(2):
                     for xs in range(2):
                         tile = acc[k * KEYS:(k + 1) * KEYS, xs * BLK:(xs + 1) * BLK]

time: 78 us -> 78 us (level)
  no operation moved by 1% of the time
where the time goes in v7:
time: 78 us; the launch traced here: 77.7 us
  Pallas kernels  72.5 us (93%)
  other arithmetic  3.91 us (5%)
    pallas_call x1, Pallas kernels, on_device(): pl.pallas_call(kernel, out_shape=[jax.ShapeDtypeStruct((BLK, WIDTH), BF16...  72.5 us
    convert_element_type x1, other arithmetic, on_device(): return (hom[None], db.astype(F32))  3.91 us

profile of v7, /device:TPU:1, one launch (start us, length us, event | category | flops | bytes accessed | tf_op | source)
XLA Modules:
  0.0 77.7 jit_solution(8659825569680348000)
XLA Ops:
  0.6 72.5 %shard_map.95 = (bf16[128,256]{1,0:T(8,128)(2,1)}, bf16[8,1024,128]{2,1,0:T(8,128)(2,1)}) custom-call(bf16[128,256]{1,0:T(8,128)(2,1)} %bitcast.4, bf16[128,256]{1,0:T(8,128)(2,1)} %bitcast.5, bf16[256,256]{1,0:T(8,128)(2,1)} %wq_ref.1, bf16[256,256]{1,0:T(8,128)(2,1)} %wk_ref.1, bf16[256,256]{1,0:T(8,128)(2,1)} %wv_ref.1, bf16[256,256]{1,0:T(8,128)(2,1)} %wg_ref.1, ...), custom_call_target="tpu_custom_call" | custom-call | flops 3000000000 | bytes 10000000 | tf_op jit(solution)/shard_map/pallas_call | solution.py:468
  73.1 0.0 copy-start
  73.1 3.9 %convert_element_type.3 = f32[8,1024,128]{2,1,0:T(8,128)} convert(bf16[8,1024,128]{2,1,0:T(8,128)(2,1)} %get-tuple-element.5) | non-fusion elementwise | flops 1048576 | bytes 6291456 | tf_op jit(solution)/shard_map/convert_element_type | solution.py:526
  77.1 0.0 copy-done
  77.1 0.6 copy.11
Async XLA Ops:
  73.1 3.9 %copy-start = (bf16[128,256]{1,0:T(8,128)(2,1)S(1)}, bf16[128,256]{1,0:T(8,128)(2,1)}, u32[]{:S(2)}) copy-start(bf16[128,256]{1,0:T(8,128)(2,1)} %get-tuple-element.4) | copy-start | bytes 196612
